TPU v7x, 512 devices: a whole 4x4x16 slice. The times are simulated.
512 devices in a mesh: gx: 64 (over x_lo, z, core), gy: 8 (over x_hi, y).
Axes of the slice: x: 4 (x_hi: 2, x_lo: 2; x = x_hi * 2 + x_lo), y: 4, z: 16, core: 2. Of those that a mesh axis runs over, the one named last changes fastest.
Arguments:
- features: bfloat16 [512, 64, 1, 8, 128], P('gx', 'gy'), may hold values from -6 to 6
- occupancy: int32 [512, 64, 1], P('gx', 'gy'), may hold values from 0 to 255
- neighbours: int32 [64, 8, 1, 27], P('gx', 'gy'), may hold values from -1 to 0, as said below
- first_weight: bfloat16 [27, 128, 128], replicated, may hold values from -0.109375 to 0.109375
- second_weight: bfloat16 [27, 128, 128], replicated, may hold values from -0.109375 to 0.109375
- cotangent: bfloat16 [512, 64, 1, 8, 128], P('gx', 'gy'), may hold values from -6 to 6
Outputs:
- activations: bfloat16 [512, 64, 1, 8, 128], P('gx', 'gy')
- first_grad: bfloat16 [27, 128, 128], replicated
- second_grad: bfloat16 [27, 128, 128], replicated
Inputs may be any that keep to these rules, and one draw needn't show every extreme that they name: `occupancy`: bit k of an entry says whether voxel layer k of that block row is occupied. `neighbours`: entry 9 (i + 1) + 3 (j + 1) + (l + 1) of slot t in column (a, b) names the slot of column (a + i, b + j) whose block lies l block layers above slot t's block, or -1 when no active block is there, the column lies outside the grid, or slot t is empty. Entry 13 is t for an active slot and -1 for an empty one; active slots come first in a column; the blocks of a column lie at distinct layers among 8; in every draw some column has all 1 slots active.
All inputs are finite; a program needn't handle non-finite values.
Results may differ from a plain program's by a relative error of at most 0.0054.
Values may be sent and summed in bfloat16 or wider, within the bound.
No kernel may reach another device: no remote copies, remote signals or barrier semaphores. Data moves between devices by JAX's collectives and lax.ppermute only.
A program may use at most 64 MiB of HBM per device.

v0:
```python
import math

import jax
import jax.numpy as jnp
from jax import lax
from jax.sharding import PartitionSpec as P


def padded(array, sides, width):
    for axis, dim in sides:
        count, length = (lax.axis_size(axis), array.shape[dim])
        up = [(i, (i + 1) % count) for i in range(count - 1)]
        down = [(j, i) for i, j in up]
        last = lax.slice_in_dim(array, length - width, length, axis=dim)
        first = lax.slice_in_dim(array, 0, width, axis=dim)
        before = lax.ppermute(last, axis, up)
        after = lax.ppermute(first, axis, down)
        array = jnp.concatenate([before, array, after], axis=dim)
    return array


def extend(window, lookup):
    extent = window.shape[0] - 2
    side_ranges = [(0, 1), (1, extent + 1), (extent + 1, extent + 2)]
    z_ranges = [(extent - 1, extent), (0, extent), (0, 1)]
    x_parts = []
    for x_part in range(3):
        y_parts = []
        for y_part in range(3):
            region = window[
                side_ranges[x_part][0] : side_ranges[x_part][1],
                side_ranges[y_part][0] : side_ranges[y_part][1],
            ]
            z_parts = []
            for z_part in range(3):
                source = lookup[:, 9 * x_part + 3 * y_part + z_part]
                layers = region[:, :, :, z_ranges[z_part][0] : z_ranges[z_part][1]]
                gathered = jnp.take(layers, jnp.maximum(source, 0), axis=2)
                present = (source >= 0).astype(window.dtype)
                z_parts.append(gathered * present[None, None, :, None, None])
            y_parts.append(jnp.concatenate(z_parts, axis=3))
        x_parts.append(jnp.concatenate(y_parts, axis=1))
    return jnp.concatenate(x_parts, axis=0)


def gather_taps(extended):
    extent = extended.shape[3] - 2
    columns = []
    for x_shift in range(3):
        for y_shift in range(3):
            for z_shift in range(3):
                columns.append(
                    extended[
                        x_shift : x_shift + extent,
                        y_shift : y_shift + extent,
                        :,
                        z_shift : z_shift + extent,
                        :,
                    ]
                )
    return jnp.concatenate(columns, axis=-1)


def flat_product(patches, weight):
    shape = patches.shape
    result = jnp.dot(patches.reshape(-1, shape[-1]), weight, preferred_element_type=jnp.float32)
    return result.reshape(shape[:-1] + (weight.shape[1],))


def outer_sum(patches, grads):
    return lax.dot_general(
        patches.reshape(-1, patches.shape[-1]),
        grads.reshape(-1, grads.shape[-1]),
        (((0,), (0,)), ((), ())),
        preferred_element_type=jnp.float32,
    )


def silu_slope(pre):
    logistic = jax.nn.sigmoid(pre)
    return logistic * (1.0 + pre * (1.0 - logistic))


def occupancy_mask(occupancy, live_cells, extent):
    bit_values = jnp.right_shift(occupancy[..., None], jnp.arange(extent, dtype=jnp.int32)) & 1
    return (bit_values * live_cells[..., None].astype(jnp.int32)).astype(jnp.bfloat16)


def boundary(volume):
    return padded(volume, (("gx", 0), ("gy", 1)), 1)


def local(features, occupancy, neighbours, first_weight, second_weight, cotangent):
    channels = features.shape[-1]
    extent = features.shape[3]
    slot_count = features.shape[2]
    lookup = neighbours[0, 0]
    live = lookup[:, 13] >= 0
    mask = occupancy_mask(occupancy, jnp.broadcast_to(live[None, None, :], occupancy.shape), extent)
    masked = features * mask[..., None]
    grad_out = cotangent * mask[..., None]
    first_flat = first_weight.reshape(27 * channels, channels)
    second_flat = second_weight.reshape(27 * channels, channels)
    second_back = jnp.transpose(second_weight[::-1], (0, 2, 1)).reshape(27 * channels, channels)
    scale = 1.0 / math.sqrt(extent**3 * slot_count * lax.axis_size("gx") * lax.axis_size("gy"))
    patches_in = gather_taps(extend(boundary(masked), lookup))
    pre_first = flat_product(patches_in, first_flat)
    hidden = (jax.nn.silu(pre_first) * mask[..., None]).astype(jnp.bfloat16)
    patches_hidden = gather_taps(extend(boundary(hidden), lookup))
    pre_second = flat_product(patches_hidden, second_flat)
    activations = (pre_second * mask[..., None]).astype(jnp.bfloat16)
    second_total = outer_sum(patches_hidden, grad_out)
    back = flat_product(gather_taps(extend(boundary(grad_out), lookup)), second_back)
    grad_pre = (back * silu_slope(pre_first) * mask[..., None]).astype(jnp.bfloat16)
    first_total = outer_sum(patches_in, grad_pre)
    first_total, second_total = lax.psum((first_total, second_total), ("gx", "gy"))
    first_grad = (first_total * scale).reshape(27, channels, channels).astype(jnp.bfloat16)
    second_grad = (second_total * scale).reshape(27, channels, channels).astype(jnp.bfloat16)
    return (activations, first_grad, second_grad)


def solution(mesh):
    in_specs = (
        P("gx", "gy", None, None, None),
        P("gx", "gy", None),
        P("gx", "gy", None, None),
        P(),
        P(),
        P("gx", "gy", None, None, None),
    )
    out_specs = (P("gx", "gy", None, None, None), P(), P())
    return jax.shard_map(local, mesh=mesh, in_specs=in_specs, out_specs=out_specs, check_vma=False)
```

profile of v0, /device:TPU:1, one launch (start us, length us, event | category | flops | bytes accessed | tf_op | source)
XLA Modules:
  0.0 625.3 jit_solution(10369003832049968784)
XLA Ops:
  7.2 1.6 fusion.97
  10.9 1.1 select_multiply_fusion
  12.0 8.8 %collective-permute-start.1 = (bf16[1,8,1,8,128]{4,3,1,0,2:T(8,128)(2,1)S(1)}, bf16[1,8,1,8,128]{4,3,1,0,2:T(8,128)(2,1)S(1)}, u32[]{:S(2)}, u32[]{:S(2)}) collective-permute-start(bf16[1,8,1,8,128]{4,3,1,0,2:T(8,128)(2,1)S(1)} %get-tuple-element.72), channel_id=1, source_target_pairs={{8,0},{16,8},{24,16},{32,24},{40,32},{48,40},{56,48},{64,56},{72,6... | collective-permute-start | bytes 49160 | tf_op jit(solution)/shard_map/ppermute | solution.py:17
  20.8 1.9 collective-permute-start
  22.8 2.4 collective-permute-start.9
  25.2 3.2 collective-permute-start.8
  28.4 2.1 fusion.96
  63.6 1.9 copy.14
  65.6 1.3 collective-permute-start.3
  66.9 4.0 collective-permute-start.2
  71.0 1.3 collective-permute-start.11
  72.3 4.0 collective-permute-start.10
  80.8 1.1 fusion.98
  82.1 2.3 collective-permute-start.5
  84.3 3.5 collective-permute-start.4
  90.6 1.7 copy-done.5
  92.4 8.1 %convolution_bitcast_fusion.1 = f32[3456,128]{1,0:T(8,128)} fusion(bf16[8,8,1,8,3456]{4,3,1,0,2:T(8,128)(2,1)} %copy-done.4, bf16[8,8,8,3456]{3,2,1,0:T(8,128)(2,1)} %copy-done.5, bf16[3456,128,1,1]{1,0,3,2:T(8,128)(2,1)S(1)} %bitcast.299, f32[8,8,8,128]{3,2,1,0:T(8,128)S(1)} %bitcast.298, f32[8,8,8]{2,1,0:T(8,128)S(1)} %get-tuple-element.136), kind=kOutput, calls=%fused_computation.1 | convolution fusion | flops 906625024 | bytes 9996288 | tf_op jit(solution)/shard_map/dot_general | solution.py:71
  100.6 1.3 collective-permute-start.7
  101.9 4.2 collective-permute-start.6
  111.5 2.7 convolution_bitcast_fusion
  119.2 3.7 fusion.5
  123.0 491.8 %all-reduce.3.cloned.1.call-done = (f32[3456,128]{1,0:T(8,128)}, f32[3456,128]{1,0:T(8,128)}) async-done(((f32[3456,128]{1,0:T(8,128)}, f32[3456,128]{1,0:T(8,128)}), (f32[3456,128]{1,0:T(8,128)}, f32[3456,128]{1,0:T(8,128)})) %all-reduce.3.cloned.1.call-update) | async-done | bytes 3538960 | tf_op jit(solution)/shard_map/psum | solution.py:116
  614.8 2.6 multiply_convert_fusion.1
  617.4 1.0 multiply_convert_fusion
  (216 shorter events, 18.0 us)
Async XLA Ops:
  7.2 73.6 %copy-start = (bf16[27,128,128]{2,1,0:T(8,128)(2,1)S(1)}, bf16[27,128,128]{2,1,0:T(8,128)(2,1)}, u32[]{:S(2)}) copy-start(bf16[27,128,128]{2,1,0:T(8,128)(2,1)} %param.9) | copy-start | bytes 2654212
  7.2 607.6 %all-reduce.3.cloned.1.call-start = ((), (), s32[]{:S(2)}) async-start(), calls=%async_computation | async-start | bytes 7077888 | tf_op jit(solution)/shard_map/psum | solution.py:116
  12.0 53.5 %collective-permute-start.1 = (bf16[1,8,1,8,128]{4,3,1,0,2:T(8,128)(2,1)S(1)}, bf16[1,8,1,8,128]{4,3,1,0,2:T(8,128)(2,1)S(1)}, u32[]{:S(2)}, u32[]{:S(2)}) collective-permute-start(bf16[1,8,1,8,128]{4,3,1,0,2:T(8,128)(2,1)S(1)} %get-tuple-element.72), channel_id=1, source_target_pairs={{8,0},{16,8},{24,16},{32,24},{40,32},{48,40},{56,48},{64,56},{72,6... | collective-permute-start | bytes 49160 | tf_op jit(solution)/shard_map/ppermute | solution.py:17
  20.8 44.7 %collective-permute-start = (bf16[1,8,1,8,128]{4,3,1,0,2:T(8,128)(2,1)S(1)}, bf16[1,8,1,8,128]{4,3,1,0,2:T(8,128)(2,1)S(1)}, u32[]{:S(2)}, u32[]{:S(2)}) collective-permute-start(bf16[1,8,1,8,128]{4,3,1,0,2:T(8,128)(2,1)S(1)} %get-tuple-element.71), channel_id=1, source_target_pairs={{0,8},{8,16},{16,24},{24,32},{32,40},{40,48},{48,56},{56,64},{64,7... | collective-permute-start | bytes 49160 | tf_op jit(solution)/shard_map/ppermute | solution.py:16
  22.8 48.1 %collective-permute-start.9 = (bf16[1,8,1,8,128]{4,3,1,0,2:T(8,128)(2,1)S(1)}, bf16[1,8,1,8,128]{4,3,1,0,2:T(8,128)(2,1)S(1)}, u32[]{:S(2)}, u32[]{:S(2)}) collective-permute-start(bf16[1,8,1,8,128]{4,3,1,0,2:T(8,128)(2,1)S(1)} %get-tuple-element.64), channel_id=1, source_target_pairs={{8,0},{16,8},{24,16},{32,24},{40,32},{48,40},{56,48},{64,56},{72,6... | collective-permute-start | bytes 49160 | tf_op jit(solution)/shard_map/ppermute | solution.py:17
  25.2 45.7 %collective-permute-start.8 = (bf16[1,8,1,8,128]{4,3,1,0,2:T(8,128)(2,1)S(1)}, bf16[1,8,1,8,128]{4,3,1,0,2:T(8,128)(2,1)S(1)}, u32[]{:S(2)}, u32[]{:S(2)}) collective-permute-start(bf16[1,8,1,8,128]{4,3,1,0,2:T(8,128)(2,1)S(1)} %get-tuple-element.63), channel_id=1, source_target_pairs={{0,8},{8,16},{16,24},{24,32},{32,40},{40,48},{48,56},{56,64},{64,7... | collective-permute-start | bytes 49160 | tf_op jit(solution)/shard_map/ppermute | solution.py:16
  65.6 10.8 %collective-permute-start.3 = (bf16[10,1,1,8,128]{4,3,1,0,2:T(8,128)(2,1)S(1)}, bf16[10,1,1,8,128]{4,3,1,0,2:T(8,128)(2,1)S(1)}, u32[]{:S(2)}, u32[]{:S(2)}) collective-permute-start(bf16[10,1,1,8,128]{4,3,1,0,2:T(8,128)(2,1)S(1)} %get-tuple-element.60), channel_id=1, source_target_pairs={{1,0},{2,1},{3,2},{4,3},{5,4},{6,5},{7,6},{9,8},{10,9},{11,10},{12... | collective-permute-start | bytes 61448 | tf_op jit(solution)/shard_map/ppermute | solution.py:17
  66.9 9.5 %collective-permute-start.2 = (bf16[10,1,1,8,128]{4,3,1,0,2:T(8,128)(2,1)S(1)}, bf16[10,1,1,8,128]{4,3,1,0,2:T(8,128)(2,1)S(1)}, u32[]{:S(2)}, u32[]{:S(2)}) collective-permute-start(bf16[10,1,1,8,128]{4,3,1,0,2:T(8,128)(2,1)S(1)} %get-tuple-element.59), channel_id=1, source_target_pairs={{0,1},{1,2},{2,3},{3,4},{4,5},{5,6},{6,7},{8,9},{9,10},{10,11},{11... | collective-permute-start | bytes 61448 | tf_op jit(solution)/shard_map/ppermute | solution.py:16
  71.0 16.9 %collective-permute-start.11 = (bf16[10,1,1,8,128]{4,3,1,0,2:T(8,128)(2,1)S(1)}, bf16[10,1,1,8,128]{4,3,1,0,2:T(8,128)(2,1)S(1)}, u32[]{:S(2)}, u32[]{:S(2)}) collective-permute-start(bf16[10,1,1,8,128]{4,3,1,0,2:T(8,128)(2,1)S(1)} %get-tuple-element.56), channel_id=1, source_target_pairs={{1,0},{2,1},{3,2},{4,3},{5,4},{6,5},{7,6},{9,8},{10,9},{11,10},{12... | collective-permute-start | bytes 61448 | tf_op jit(solution)/shard_map/ppermute | solution.py:17
  72.3 15.6 %collective-permute-start.10 = (bf16[10,1,1,8,128]{4,3,1,0,2:T(8,128)(2,1)S(1)}, bf16[10,1,1,8,128]{4,3,1,0,2:T(8,128)(2,1)S(1)}, u32[]{:S(2)}, u32[]{:S(2)}) collective-permute-start(bf16[10,1,1,8,128]{4,3,1,0,2:T(8,128)(2,1)S(1)} %get-tuple-element.55), channel_id=1, source_target_pairs={{0,1},{1,2},{2,3},{3,4},{4,5},{5,6},{6,7},{8,9},{9,10},{10,11},{11... | collective-permute-start | bytes 61448 | tf_op jit(solution)/shard_map/ppermute | solution.py:16
  79.7 2.2 copy-start.4
  82.1 18.5 %collective-permute-start.5 = (bf16[1,8,1,8,128]{4,3,1,0,2:T(8,128)(2,1)S(1)}, bf16[1,8,1,8,128]{4,3,1,0,2:T(8,128)(2,1)S(1)}, u32[]{:S(2)}, u32[]{:S(2)}) collective-permute-start(bf16[1,8,1,8,128]{4,3,1,0,2:T(8,128)(2,1)S(1)} %get-tuple-element.68), channel_id=1, source_target_pairs={{8,0},{16,8},{24,16},{32,24},{40,32},{48,40},{56,48},{64,56},{72,6... | collective-permute-start | bytes 49160 | tf_op jit(solution)/shard_map/ppermute | solution.py:17
  84.3 16.3 %collective-permute-start.4 = (bf16[1,8,1,8,128]{4,3,1,0,2:T(8,128)(2,1)S(1)}, bf16[1,8,1,8,128]{4,3,1,0,2:T(8,128)(2,1)S(1)}, u32[]{:S(2)}, u32[]{:S(2)}) collective-permute-start(bf16[1,8,1,8,128]{4,3,1,0,2:T(8,128)(2,1)S(1)} %get-tuple-element.67), channel_id=1, source_target_pairs={{0,8},{8,16},{16,24},{24,32},{32,40},{40,48},{48,56},{56,64},{64,7... | collective-permute-start | bytes 49160 | tf_op jit(solution)/shard_map/ppermute | solution.py:16
  90.6 1.7 copy-start.5
  100.6 5.6 collective-permute-start.7
  101.9 4.9 collective-permute-start.6
  109.1 1.7 copy-start.1
  114.2 5.0 copy-start.2
  614.8 2.6 copy-start.3
Sparse Core Ops, SparseCore 0:
  114.4 500.3 all-reduce.2
where the time goes:
time: 627 us; the launch traced here: 625 us
  waiting for transfers between devices  492 us (78%)
  between operations  49.6 us (8%)
  starting transfers between devices  38.1 us (6%)
  local copies, waits for them, and re-layouts  19.8 us (3%)
  matrix products  15.7 us (3%)
  other arithmetic  9.65 us (2%)
    psum x1, waiting for transfers between devices, local(): lax.psum((first_total, second_total), ('gx', 'gy'))  492 us
    ppermute x6, starting transfers between devices, padded(): before = lax.ppermute(last, axis, up)  20.8 us
    ppermute x6, starting transfers between devices, padded(): after = lax.ppermute(first, axis, down)  17.3 us
    unnamed x135, local copies, waits for them, and re-layouts  14.9 us
  transfers between devices with their start and end apart: 13, of which 2 were waited for; matrix products, arithmetic and copies ran while one was open for 5% of the time, Pallas kernels for 0%

commit v1 on v0

--- a/solution.py
+++ b/solution.py
@@ -3,7 +3,11 @@
 import jax
 import jax.numpy as jnp
 from jax import lax
+from jax.sharding import Mesh
 from jax.sharding import PartitionSpec as P
+
+GX = ("x_lo", "z", "core")
+GY = ("x_hi", "y")
 
 
 def padded(array, sides, width):
@@ -87,7 +91,41 @@
 
 
 def boundary(volume):
-    return padded(volume, (("gx", 0), ("gy", 1)), 1)
+    return padded(volume, ((GX, 0), (GY, 1)), 1)
+
+
+def exchange(parts, axes):
+    return lax.all_to_all(parts, axes, 0, 0, tiled=True)
+
+
+def summed(parts):
+    return jnp.sum(parts.astype(jnp.float32), axis=0).astype(jnp.bfloat16)
+
+
+def shared(part, count):
+    return jnp.broadcast_to(part[None], (count,) + part.shape)
+
+
+def reduced(first_total, second_total, scale):
+    core = lax.axis_index("core")
+    swap = [(0, 1), (1, 0)]
+    plane = ("x_lo", "x_hi", "y")
+    along = ("z",)
+    plane_count, along_count = (lax.axis_size(plane), lax.axis_size(along))
+    keep = jnp.where(core == 0, first_total, second_total)
+    send = jnp.where(core == 0, second_total, first_total).astype(jnp.bfloat16)
+    half = (keep + lax.ppermute(send, "core", swap).astype(jnp.float32)).astype(jnp.bfloat16)
+    rows, channels = half.shape
+    piece = rows // plane_count
+    unit = -(-piece // (16 * along_count)) * 16
+    part = summed(exchange(half.reshape(plane_count, piece, channels), plane))
+    part = jnp.pad(part, ((0, unit * along_count - piece), (0, 0)))
+    part = exchange(part.reshape(along_count, unit, channels), along)
+    part = (jnp.sum(part.astype(jnp.float32), axis=0) * scale).astype(jnp.bfloat16)
+    part = exchange(shared(part, along_count), along).reshape(-1, channels)[:piece]
+    half = exchange(shared(part, plane_count), plane).reshape(rows, channels)
+    other = lax.ppermute(half, "core", swap)
+    return jnp.where(core == 0, half, other), jnp.where(core == 0, other, half)
 
 
 def local(features, occupancy, neighbours, first_weight, second_weight, cotangent):
@@ -102,7 +140,7 @@
     first_flat = first_weight.reshape(27 * channels, channels)
     second_flat = second_weight.reshape(27 * channels, channels)
     second_back = jnp.transpose(second_weight[::-1], (0, 2, 1)).reshape(27 * channels, channels)
-    scale = 1.0 / math.sqrt(extent**3 * slot_count * lax.axis_size("gx") * lax.axis_size("gy"))
+    scale = 1.0 / math.sqrt(extent**3 * slot_count * lax.axis_size(GX) * lax.axis_size(GY))
     patches_in = gather_taps(extend(boundary(masked), lookup))
     pre_first = flat_product(patches_in, first_flat)
     hidden = (jax.nn.silu(pre_first) * mask[..., None]).astype(jnp.bfloat16)
@@ -113,20 +151,21 @@
     back = flat_product(gather_taps(extend(boundary(grad_out), lookup)), second_back)
     grad_pre = (back * silu_slope(pre_first) * mask[..., None]).astype(jnp.bfloat16)
     first_total = outer_sum(patches_in, grad_pre)
-    first_total, second_total = lax.psum((first_total, second_total), ("gx", "gy"))
-    first_grad = (first_total * scale).reshape(27, channels, channels).astype(jnp.bfloat16)
-    second_grad = (second_total * scale).reshape(27, channels, channels).astype(jnp.bfloat16)
+    first_total, second_total = reduced(first_total, second_total, scale)
+    first_grad = first_total.reshape(27, channels, channels)
+    second_grad = second_total.reshape(27, channels, channels)
     return (activations, first_grad, second_grad)
 
 
 def solution(mesh):
+    fine = Mesh(mesh.devices.reshape(2, 16, 2, 2, 4), GX + GY)
     in_specs = (
-        P("gx", "gy", None, None, None),
-        P("gx", "gy", None),
-        P("gx", "gy", None, None),
+        P(GX, GY, None, None, None),
+        P(GX, GY, None),
+        P(GX, GY, None, None),
         P(),
         P(),
-        P("gx", "gy", None, None, None),
+        P(GX, GY, None, None, None),
     )
-    out_specs = (P("gx", "gy", None, None, None), P(), P())
-    return jax.shard_map(local, mesh=mesh, in_specs=in_specs, out_specs=out_specs, check_vma=False)
+    out_specs = (P(GX, GY, None, None, None), P(), P())
+    return jax.shard_map(local, mesh=fine, in_specs=in_specs, out_specs=out_specs, check_vma=False)

time: 627 us -> 222 us (0.35)
  waiting for transfers between devices: 492 us -> 39.5 us
  starting transfers between devices: 38.1 us -> 87 us
  local copies, waits for them, and re-layouts: 19.8 us -> 33.2 us
  between operations: 49.6 us -> 36.3 us
    psum x1 -> x0, waiting for transfers between devices: 492 us -> none  [local(): lax.psum((first_total, second_total), ('gx', 'gy'))]
    all_to_all x0 -> x4, starting transfers between devices: none -> 39.7 us  [exchange(): return lax.all_to_all(parts, axes, 0, 0, tiled=True)]
    all_to_all x0 -> x4, waiting for transfers between devices: none -> 38.7 us  [exchange(): return lax.all_to_all(parts, axes, 0, 0, tiled=True)]
    unnamed x135 -> x131, local copies, waits for them, and re-layouts: 14.9 us -> 26 us
    ppermute x0 -> x2, starting transfers between devices: none -> 9.48 us  [the longest x1 7.32 us: reduced(): other = lax.ppermute(half, 'core', swap)]
  transfers between devices with their start and end apart: 13 -> 18, of which waited for: 2 -> 5; matrix products, arithmetic and copies ran while one was open for 5% -> 18% of each run, Pallas kernels for 0% -> 0%
where the time goes in v1:
time: 222 us; the launch traced here: 221 us
  starting transfers between devices  87 us (39%)
  waiting for transfers between devices  39.5 us (18%)
  between operations  36.3 us (16%)
  local copies, waits for them, and re-layouts  33.2 us (15%)
  matrix products  14.7 us (7%)
  other arithmetic  10 us (5%)
    all_to_all x4, starting transfers between devices, exchange(): return lax.all_to_all(parts, axes, 0, 0, tiled=True)  39.7 us
    all_to_all x4, waiting for transfers between devices, exchange(): return lax.all_to_all(parts, axes, 0, 0, tiled=True)  38.7 us
    unnamed x131, local copies, waits for them, and re-layouts  26 us
    ppermute x6, starting transfers between devices, padded(): before = lax.ppermute(last, axis, up)  20.5 us
    ppermute x6, starting transfers between devices, padded(): after = lax.ppermute(first, axis, down)  17.3 us
    dot_general x2, matrix products, outer_sum(): lax.dot_general(patches.reshape(-1, patches.shape[-1]), grads.reshape(-1,...  9.68 us
    ppermute x1, starting transfers between devices, reduced(): other = lax.ppermute(half, 'core', swap)  7.32 us
    dot_general x2, matrix products, flat_product(): jnp.dot(patches.reshape(-1, shape[-1]), weight, preferred_element_type=jn...  5.06 us
  transfers between devices with their start and end apart: 18, of which 5 were waited for; matrix products, arithmetic and copies ran while one was open for 18% of the time, Pallas kernels for 0%

profile of v1, /device:TPU:1, one launch (start us, length us, event | category | flops | bytes accessed | tf_op | source)
XLA Modules:
  0.0 220.8 jit_solution(7663708433863070473)
XLA Ops:
  5.5 8.8 %collective-permute-start.1 = (bf16[1,8,1,8,128]{4,3,1,0,2:T(8,128)(2,1)S(1)}, bf16[1,8,1,8,128]{4,3,1,0,2:T(8,128)(2,1)S(1)}, u32[]{:S(2)}, u32[]{:S(2)}) collective-permute-start(bf16[1,8,1,8,128]{4,3,1,0,2:T(8,128)(2,1)S(1)} %get-tuple-element.75), channel_id=1, source_target_pairs={{8,0},{16,8},{24,16},{32,24},{40,32},{48,40},{56,48},{64,56},{72,6... | collective-permute-start | bytes 49160 | tf_op jit(solution)/shard_map/ppermute | solution.py:21
  14.3 1.9 collective-permute-start
  16.2 2.4 %collective-permute-start.9 = (bf16[1,8,1,8,128]{4,3,1,0,2:T(8,128)(2,1)S(1)}, bf16[1,8,1,8,128]{4,3,1,0,2:T(8,128)(2,1)S(1)}, u32[]{:S(2)}, u32[]{:S(2)}) collective-permute-start(bf16[1,8,1,8,128]{4,3,1,0,2:T(8,128)(2,1)S(1)} %get-tuple-element.67), channel_id=1, source_target_pairs={{8,0},{16,8},{24,16},{32,24},{40,32},{48,40},{56,48},{64,56},{72,6... | collective-permute-start | bytes 49160 | tf_op jit(solution)/shard_map/ppermute | solution.py:21
  18.6 3.2 %collective-permute-start.8 = (bf16[1,8,1,8,128]{4,3,1,0,2:T(8,128)(2,1)S(1)}, bf16[1,8,1,8,128]{4,3,1,0,2:T(8,128)(2,1)S(1)}, u32[]{:S(2)}, u32[]{:S(2)}) collective-permute-start(bf16[1,8,1,8,128]{4,3,1,0,2:T(8,128)(2,1)S(1)} %get-tuple-element.66), channel_id=1, source_target_pairs={{0,8},{8,16},{16,24},{24,32},{32,40},{40,48},{48,56},{56,64},{64,7... | collective-permute-start | bytes 49160 | tf_op jit(solution)/shard_map/ppermute | solution.py:20
  21.8 2.1 fusion.96
  57.1 1.9 copy.18
  60.4 4.0 %collective-permute-start.2 = (bf16[10,1,1,8,128]{4,3,1,0,2:T(8,128)(2,1)S(1)}, bf16[10,1,1,8,128]{4,3,1,0,2:T(8,128)(2,1)S(1)}, u32[]{:S(2)}, u32[]{:S(2)}) collective-permute-start(bf16[10,1,1,8,128]{4,3,1,0,2:T(8,128)(2,1)S(1)} %get-tuple-element.62), channel_id=1, source_target_pairs={{0,1},{1,2},{2,3},{3,4},{4,5},{5,6},{6,7},{8,9},{9,10},{10,11},{11... | collective-permute-start | bytes 61448 | tf_op jit(solution)/shard_map/ppermute | solution.py:20
  65.8 4.0 %collective-permute-start.10 = (bf16[10,1,1,8,128]{4,3,1,0,2:T(8,128)(2,1)S(1)}, bf16[10,1,1,8,128]{4,3,1,0,2:T(8,128)(2,1)S(1)}, u32[]{:S(2)}, u32[]{:S(2)}) collective-permute-start(bf16[10,1,1,8,128]{4,3,1,0,2:T(8,128)(2,1)S(1)} %get-tuple-element.58), channel_id=1, source_target_pairs={{0,1},{1,2},{2,3},{3,4},{4,5},{5,6},{6,7},{8,9},{9,10},{10,11},{11... | collective-permute-start | bytes 61448 | tf_op jit(solution)/shard_map/ppermute | solution.py:20
  75.6 2.3 %collective-permute-start.5 = (bf16[1,8,1,8,128]{4,3,1,0,2:T(8,128)(2,1)S(1)}, bf16[1,8,1,8,128]{4,3,1,0,2:T(8,128)(2,1)S(1)}, u32[]{:S(2)}, u32[]{:S(2)}) collective-permute-start(bf16[1,8,1,8,128]{4,3,1,0,2:T(8,128)(2,1)S(1)} %get-tuple-element.71), channel_id=1, source_target_pairs={{8,0},{16,8},{24,16},{32,24},{40,32},{48,40},{56,48},{64,56},{72,6... | collective-permute-start | bytes 49160 | tf_op jit(solution)/shard_map/ppermute | solution.py:21
  77.8 3.5 %collective-permute-start.4 = (bf16[1,8,1,8,128]{4,3,1,0,2:T(8,128)(2,1)S(1)}, bf16[1,8,1,8,128]{4,3,1,0,2:T(8,128)(2,1)S(1)}, u32[]{:S(2)}, u32[]{:S(2)}) collective-permute-start(bf16[1,8,1,8,128]{4,3,1,0,2:T(8,128)(2,1)S(1)} %get-tuple-element.70), channel_id=1, source_target_pairs={{0,8},{8,16},{16,24},{24,32},{32,40},{40,48},{48,56},{56,64},{64,7... | collective-permute-start | bytes 49160 | tf_op jit(solution)/shard_map/ppermute | solution.py:20
  84.1 1.7 copy-done.3
  85.9 8.1 %convolution_bitcast_fusion.1 = f32[3456,128]{1,0:T(8,128)} fusion(bf16[8,8,1,8,3456]{4,3,1,0,2:T(8,128)(2,1)} %copy-done.2, bf16[8,8,8,3456]{3,2,1,0:T(8,128)(2,1)} %copy-done.3, bf16[3456,128,1,1]{1,0,3,2:T(8,128)(2,1)S(1)} %bitcast.311, f32[8,8,8,128]{3,2,1,0:T(8,128)S(1)} %bitcast.310, f32[8,8,8]{2,1,0:T(8,128)S(1)} %get-tuple-element.139), kind=kOutput, calls=%fused_computation.1 | convolution fusion | flops 906625024 | bytes 9996288 | tf_op jit(solution)/shard_map/dot_general | solution.py:75
  95.4 4.0 %collective-permute-start.6 = (bf16[10,1,1,8,128]{4,3,1,0,2:T(8,128)(2,1)S(1)}, bf16[10,1,1,8,128]{4,3,1,0,2:T(8,128)(2,1)S(1)}, u32[]{:S(2)}, u32[]{:S(2)}) collective-permute-start(bf16[10,1,1,8,128]{4,3,1,0,2:T(8,128)(2,1)S(1)} %get-tuple-element.60), channel_id=1, source_target_pairs={{0,1},{1,2},{2,3},{3,4},{4,5},{5,6},{6,7},{8,9},{9,10},{10,11},{11... | collective-permute-start | bytes 61448 | tf_op jit(solution)/shard_map/ppermute | solution.py:20
  109.6 2.2 collective-permute-start.12
  115.8 27.5 %all-to-all-start = ((bf16[16,216,128]{2,1,0:T(8,128)(2,1)}), bf16[16,216,128]{2,1,0:T(8,128)(2,1)S(1)}, u32[]{:S(2)}, u32[]{:S(2)}) async-start(bf16[16,216,128]{2,1,0:T(8,128)(2,1)} %bitcast.308), calls=%async_computation | async-start | bytes 1769472 | tf_op jit(solution)/shard_map/all_to_all | solution.py:98
  146.9 10.3 %all-to-all-done = bf16[16,216,128]{2,1,0:T(8,128)(2,1)S(1)} async-done(((bf16[16,216,128]{2,1,0:T(8,128)(2,1)}), bf16[16,216,128]{2,1,0:T(8,128)(2,1)S(1)}, u32[]{:S(2)}, u32[]{:S(2)}) %all-to-all-start) | async-done | bytes 884768 | tf_op jit(solution)/shard_map/all_to_all | solution.py:98
  158.0 4.2 %all-to-all-start.1 = ((bf16[16,16,128]{2,1,0:T(8,128)(2,1)}), bf16[16,16,128]{2,1,0:T(8,128)(2,1)S(1)}, u32[]{:S(2)}, u32[]{:S(2)}) async-start(bf16[16,16,128]{2,1,0:T(8,128)(2,1)} %bitcast.162), calls=%async_computation.1 | async-start | bytes 131072 | tf_op jit(solution)/shard_map/all_to_all | solution.py:98
  163.6 10.1 %all-to-all-done.1 = bf16[16,16,128]{2,1,0:T(8,128)(2,1)S(1)} async-done(((bf16[16,16,128]{2,1,0:T(8,128)(2,1)}), bf16[16,16,128]{2,1,0:T(8,128)(2,1)S(1)}, u32[]{:S(2)}, u32[]{:S(2)}) %all-to-all-start.1) | async-done | bytes 65568 | tf_op jit(solution)/shard_map/all_to_all | solution.py:98
  174.4 3.5 %all-to-all-start.2 = ((bf16[16,16,128]{2,1,0:T(8,128)(2,1)}), bf16[16,16,128]{2,1,0:T(8,128)(2,1)S(1)}, u32[]{:S(2)}, u32[]{:S(2)}) async-start(bf16[16,16,128]{2,1,0:T(8,128)(2,1)} %broadcast_in_dim.473), calls=%async_computation.2 | async-start | bytes 131072 | tf_op jit(solution)/shard_map/all_to_all | solution.py:98
  179.4 10.2 %all-to-all-done.2 = bf16[16,16,128]{2,1,0:T(8,128)(2,1)S(1)} async-done(((bf16[16,16,128]{2,1,0:T(8,128)(2,1)}), bf16[16,16,128]{2,1,0:T(8,128)(2,1)S(1)}, u32[]{:S(2)}, u32[]{:S(2)}) %all-to-all-start.2) | async-done | bytes 65568 | tf_op jit(solution)/shard_map/all_to_all | solution.py:98
  190.6 4.5 %all-to-all-start.3 = ((bf16[16,216,128]{2,1,0:T(8,128)(2,1)}), bf16[16,216,128]{2,1,0:T(8,128)(2,1)S(1)}, u32[]{:S(2)}, u32[]{:S(2)}) async-start(bf16[16,216,128]{2,1,0:T(8,128)(2,1)} %broadcast_in_dim.474), calls=%async_computation.3 | async-start | bytes 1769472 | tf_op jit(solution)/shard_map/all_to_all | solution.py:98
  197.9 8.1 %all-to-all-done.3 = bf16[16,216,128]{2,1,0:T(8,128)(2,1)S(1)} async-done(((bf16[16,216,128]{2,1,0:T(8,128)(2,1)}), bf16[16,216,128]{2,1,0:T(8,128)(2,1)S(1)}, u32[]{:S(2)}, u32[]{:S(2)}) %all-to-all-start.3) | async-done | bytes 884768 | tf_op jit(solution)/shard_map/all_to_all | solution.py:98
  206.0 7.3 %collective-permute-start.13 = (bf16[3456,128]{1,0:T(8,128)(2,1)S(1)}, bf16[3456,128]{1,0:T(8,128)(2,1)S(1)}, u32[]{:S(2)}, u32[]{:S(2)}) collective-permute-start(bf16[3456,128]{1,0:T(8,128)(2,1)S(1)} %bitcast.306), channel_id=1, source_target_pairs={{0,8},{8,0},{1,9},{9,1},{2,10},{10,2},{3,11},{11,3},{4,12},{12,4},... | collective-permute-start | bytes 2654216 | tf_op jit(solution)/shard_map/ppermute | solution.py:127
  215.5 4.0 %fusion.5 = bf16[8,8,1,8,128]{4,3,2,1,0:T(8,128)(2,1)} fusion(bf16[8,8,8,3456]{3,2,1,0:T(8,128)(2,1)} %constant_dynamic-update-slice_fusion.27, bf16[3456,128,1,1]{1,0,3,2:T(8,128)(2,1)} %bitcast.307, f32[8,8,8]{2,1,0:T(8,128)S(1)} %get-tuple-element.139), kind=kOutput, calls=%fused_computation.11 | convolution fusion | flops 453115904 | bytes 4556800 | tf_op jit(solution)/shard_map/dot_general | solution.py:70
  (228 shorter events, 44.9 us)
Async XLA Ops:
  0.6 73.7 %copy-start = (bf16[27,128,128]{2,1,0:T(8,128)(2,1)S(1)}, bf16[27,128,128]{2,1,0:T(8,128)(2,1)}, u32[]{:S(2)}) copy-start(bf16[27,128,128]{2,1,0:T(8,128)(2,1)} %param.9) | copy-start | bytes 2654212
  5.5 53.6 %collective-permute-start.1 = (bf16[1,8,1,8,128]{4,3,1,0,2:T(8,128)(2,1)S(1)}, bf16[1,8,1,8,128]{4,3,1,0,2:T(8,128)(2,1)S(1)}, u32[]{:S(2)}, u32[]{:S(2)}) collective-permute-start(bf16[1,8,1,8,128]{4,3,1,0,2:T(8,128)(2,1)S(1)} %get-tuple-element.75), channel_id=1, source_target_pairs={{8,0},{16,8},{24,16},{32,24},{40,32},{48,40},{56,48},{64,56},{72,6... | collective-permute-start | bytes 49160 | tf_op jit(solution)/shard_map/ppermute | solution.py:21
  14.3 44.8 %collective-permute-start = (bf16[1,8,1,8,128]{4,3,1,0,2:T(8,128)(2,1)S(1)}, bf16[1,8,1,8,128]{4,3,1,0,2:T(8,128)(2,1)S(1)}, u32[]{:S(2)}, u32[]{:S(2)}) collective-permute-start(bf16[1,8,1,8,128]{4,3,1,0,2:T(8,128)(2,1)S(1)} %get-tuple-element.74), channel_id=1, source_target_pairs={{0,8},{8,16},{16,24},{24,32},{32,40},{40,48},{48,56},{56,64},{64,7... | collective-permute-start | bytes 49160 | tf_op jit(solution)/shard_map/ppermute | solution.py:20
  16.2 48.2 %collective-permute-start.9 = (bf16[1,8,1,8,128]{4,3,1,0,2:T(8,128)(2,1)S(1)}, bf16[1,8,1,8,128]{4,3,1,0,2:T(8,128)(2,1)S(1)}, u32[]{:S(2)}, u32[]{:S(2)}) collective-permute-start(bf16[1,8,1,8,128]{4,3,1,0,2:T(8,128)(2,1)S(1)} %get-tuple-element.67), channel_id=1, source_target_pairs={{8,0},{16,8},{24,16},{32,24},{40,32},{48,40},{56,48},{64,56},{72,6... | collective-permute-start | bytes 49160 | tf_op jit(solution)/shard_map/ppermute | solution.py:21
  18.6 45.8 %collective-permute-start.8 = (bf16[1,8,1,8,128]{4,3,1,0,2:T(8,128)(2,1)S(1)}, bf16[1,8,1,8,128]{4,3,1,0,2:T(8,128)(2,1)S(1)}, u32[]{:S(2)}, u32[]{:S(2)}) collective-permute-start(bf16[1,8,1,8,128]{4,3,1,0,2:T(8,128)(2,1)S(1)} %get-tuple-element.66), channel_id=1, source_target_pairs={{0,8},{8,16},{16,24},{24,32},{32,40},{40,48},{48,56},{56,64},{64,7... | collective-permute-start | bytes 49160 | tf_op jit(solution)/shard_map/ppermute | solution.py:20
  59.1 10.8 %collective-permute-start.3 = (bf16[10,1,1,8,128]{4,3,1,0,2:T(8,128)(2,1)S(1)}, bf16[10,1,1,8,128]{4,3,1,0,2:T(8,128)(2,1)S(1)}, u32[]{:S(2)}, u32[]{:S(2)}) collective-permute-start(bf16[10,1,1,8,128]{4,3,1,0,2:T(8,128)(2,1)S(1)} %get-tuple-element.63), channel_id=1, source_target_pairs={{1,0},{2,1},{3,2},{4,3},{5,4},{6,5},{7,6},{9,8},{10,9},{11,10},{12... | collective-permute-start | bytes 61448 | tf_op jit(solution)/shard_map/ppermute | solution.py:21
  60.4 9.5 %collective-permute-start.2 = (bf16[10,1,1,8,128]{4,3,1,0,2:T(8,128)(2,1)S(1)}, bf16[10,1,1,8,128]{4,3,1,0,2:T(8,128)(2,1)S(1)}, u32[]{:S(2)}, u32[]{:S(2)}) collective-permute-start(bf16[10,1,1,8,128]{4,3,1,0,2:T(8,128)(2,1)S(1)} %get-tuple-element.62), channel_id=1, source_target_pairs={{0,1},{1,2},{2,3},{3,4},{4,5},{5,6},{6,7},{8,9},{9,10},{10,11},{11... | collective-permute-start | bytes 61448 | tf_op jit(solution)/shard_map/ppermute | solution.py:20
  64.5 16.9 %collective-permute-start.11 = (bf16[10,1,1,8,128]{4,3,1,0,2:T(8,128)(2,1)S(1)}, bf16[10,1,1,8,128]{4,3,1,0,2:T(8,128)(2,1)S(1)}, u32[]{:S(2)}, u32[]{:S(2)}) collective-permute-start(bf16[10,1,1,8,128]{4,3,1,0,2:T(8,128)(2,1)S(1)} %get-tuple-element.59), channel_id=1, source_target_pairs={{1,0},{2,1},{3,2},{4,3},{5,4},{6,5},{7,6},{9,8},{10,9},{11,10},{12... | collective-permute-start | bytes 61448 | tf_op jit(solution)/shard_map/ppermute | solution.py:21
  65.8 15.6 %collective-permute-start.10 = (bf16[10,1,1,8,128]{4,3,1,0,2:T(8,128)(2,1)S(1)}, bf16[10,1,1,8,128]{4,3,1,0,2:T(8,128)(2,1)S(1)}, u32[]{:S(2)}, u32[]{:S(2)}) collective-permute-start(bf16[10,1,1,8,128]{4,3,1,0,2:T(8,128)(2,1)S(1)} %get-tuple-element.58), channel_id=1, source_target_pairs={{0,1},{1,2},{2,3},{3,4},{4,5},{5,6},{6,7},{8,9},{9,10},{10,11},{11... | collective-permute-start | bytes 61448 | tf_op jit(solution)/shard_map/ppermute | solution.py:20
  73.2 2.2 copy-start.2
  75.6 18.5 %collective-permute-start.5 = (bf16[1,8,1,8,128]{4,3,1,0,2:T(8,128)(2,1)S(1)}, bf16[1,8,1,8,128]{4,3,1,0,2:T(8,128)(2,1)S(1)}, u32[]{:S(2)}, u32[]{:S(2)}) collective-permute-start(bf16[1,8,1,8,128]{4,3,1,0,2:T(8,128)(2,1)S(1)} %get-tuple-element.71), channel_id=1, source_target_pairs={{8,0},{16,8},{24,16},{32,24},{40,32},{48,40},{56,48},{64,56},{72,6... | collective-permute-start | bytes 49160 | tf_op jit(solution)/shard_map/ppermute | solution.py:21
  77.8 16.3 %collective-permute-start.4 = (bf16[1,8,1,8,128]{4,3,1,0,2:T(8,128)(2,1)S(1)}, bf16[1,8,1,8,128]{4,3,1,0,2:T(8,128)(2,1)S(1)}, u32[]{:S(2)}, u32[]{:S(2)}) collective-permute-start(bf16[1,8,1,8,128]{4,3,1,0,2:T(8,128)(2,1)S(1)} %get-tuple-element.70), channel_id=1, source_target_pairs={{0,8},{8,16},{16,24},{24,32},{32,40},{40,48},{48,56},{56,64},{64,7... | collective-permute-start | bytes 49160 | tf_op jit(solution)/shard_map/ppermute | solution.py:20
  84.1 1.7 copy-start.3
  94.1 5.4 %collective-permute-start.7 = (bf16[10,1,1,8,128]{4,3,1,0,2:T(8,128)(2,1)S(1)}, bf16[10,1,1,8,128]{4,3,1,0,2:T(8,128)(2,1)S(1)}, u32[]{:S(2)}, u32[]{:S(2)}) collective-permute-start(bf16[10,1,1,8,128]{4,3,1,0,2:T(8,128)(2,1)S(1)} %get-tuple-element.61), channel_id=1, source_target_pairs={{1,0},{2,1},{3,2},{4,3},{5,4},{6,5},{7,6},{9,8},{10,9},{11,10},{12... | collective-permute-start | bytes 61448 | tf_op jit(solution)/shard_map/ppermute | solution.py:21
  95.4 4.9 %collective-permute-start.6 = (bf16[10,1,1,8,128]{4,3,1,0,2:T(8,128)(2,1)S(1)}, bf16[10,1,1,8,128]{4,3,1,0,2:T(8,128)(2,1)S(1)}, u32[]{:S(2)}, u32[]{:S(2)}) collective-permute-start(bf16[10,1,1,8,128]{4,3,1,0,2:T(8,128)(2,1)S(1)} %get-tuple-element.60), channel_id=1, source_target_pairs={{0,1},{1,2},{2,3},{3,4},{4,5},{5,6},{6,7},{8,9},{9,10},{10,11},{11... | collective-permute-start | bytes 61448 | tf_op jit(solution)/shard_map/ppermute | solution.py:20
  106.1 1.9 copy-start.1
  109.6 5.1 %collective-permute-start.12 = (bf16[3456,128]{1,0:T(8,128)(2,1)S(1)}, bf16[3456,128]{1,0:T(8,128)(2,1)S(1)}, u32[]{:S(2)}, u32[]{:S(2)}) collective-permute-start(bf16[3456,128]{1,0:T(8,128)(2,1)S(1)} %get-tuple-element.167), channel_id=1, source_target_pairs={{0,8},{8,0},{1,9},{9,1},{2,10},{10,2},{3,11},{11,3},{4,12},{12,4},... | collective-permute-start | bytes 2654216 | tf_op jit(solution)/shard_map/ppermute | solution.py:117
  115.8 41.4 %all-to-all-start = ((bf16[16,216,128]{2,1,0:T(8,128)(2,1)}), bf16[16,216,128]{2,1,0:T(8,128)(2,1)S(1)}, u32[]{:S(2)}, u32[]{:S(2)}) async-start(bf16[16,216,128]{2,1,0:T(8,128)(2,1)} %bitcast.308), calls=%async_computation | async-start | bytes 1769472 | tf_op jit(solution)/shard_map/all_to_all | solution.py:98
  158.0 15.8 %all-to-all-start.1 = ((bf16[16,16,128]{2,1,0:T(8,128)(2,1)}), bf16[16,16,128]{2,1,0:T(8,128)(2,1)S(1)}, u32[]{:S(2)}, u32[]{:S(2)}) async-start(bf16[16,16,128]{2,1,0:T(8,128)(2,1)} %bitcast.162), calls=%async_computation.1 | async-start | bytes 131072 | tf_op jit(solution)/shard_map/all_to_all | solution.py:98
  174.4 15.1 %all-to-all-start.2 = ((bf16[16,16,128]{2,1,0:T(8,128)(2,1)}), bf16[16,16,128]{2,1,0:T(8,128)(2,1)S(1)}, u32[]{:S(2)}, u32[]{:S(2)}) async-start(bf16[16,16,128]{2,1,0:T(8,128)(2,1)} %broadcast_in_dim.473), calls=%async_computation.2 | async-start | bytes 131072 | tf_op jit(solution)/shard_map/all_to_all | solution.py:98
  190.6 15.4 %all-to-all-start.3 = ((bf16[16,216,128]{2,1,0:T(8,128)(2,1)}), bf16[16,216,128]{2,1,0:T(8,128)(2,1)S(1)}, u32[]{:S(2)}, u32[]{:S(2)}) async-start(bf16[16,216,128]{2,1,0:T(8,128)(2,1)} %broadcast_in_dim.474), calls=%async_computation.3 | async-start | bytes 1769472 | tf_op jit(solution)/shard_map/all_to_all | solution.py:98
  206.0 13.4 %collective-permute-start.13 = (bf16[3456,128]{1,0:T(8,128)(2,1)S(1)}, bf16[3456,128]{1,0:T(8,128)(2,1)S(1)}, u32[]{:S(2)}, u32[]{:S(2)}) collective-permute-start(bf16[3456,128]{1,0:T(8,128)(2,1)S(1)} %bitcast.306), channel_id=1, source_target_pairs={{0,8},{8,0},{1,9},{9,1},{2,10},{10,2},{3,11},{11,3},{4,12},{12,4},... | collective-permute-start | bytes 2654216 | tf_op jit(solution)/shard_map/ppermute | solution.py:127

commit v2 on v0

v2 whole, which is shorter than its diff:
```python
import functools
import math

import jax
import jax.numpy as jnp
from jax import lax
from jax.experimental import pallas as pl
from jax.experimental.pallas import tpu as pltpu
from jax.sharding import Mesh
from jax.sharding import PartitionSpec as P

GX = ("x_lo", "z", "core")
GY = ("x_hi", "y")
PLANE = ("x_lo", "x_hi", "y")
ALONG = ("z",)
SWAP = [(0, 1), (1, 0)]
F32 = jnp.float32
BF16 = jnp.bfloat16
E = 8
LIMIT = 48 * 1024 * 1024
VMEM = pl.BlockSpec(memory_space=pltpu.VMEM)
SMEM = pl.BlockSpec(memory_space=pltpu.SMEM)


def column_mask(occupancy, live, x, y):
    layers = lax.broadcasted_iota(jnp.int32, (E, 128), 0)
    bits = jnp.right_shift(jnp.full((E, 128), occupancy[x, y, 0] * live, jnp.int32), layers) & 1
    return bits.astype(F32)


def row_mask(occupancy, live, x):
    return jnp.stack([column_mask(occupancy, live, x, y) for y in range(E)])


def present(neighbours, p, q):
    base = 9 * (p + 1) + 3 * (q + 1)
    return [jnp.where(neighbours[0, 0, 0, base + r] >= 0, 1.0, 0.0).astype(F32) for r in range(3)]


def live_of(neighbours):
    return jnp.where(neighbours[0, 0, 0, 13] >= 0, 1, 0)


def faces_x(features, cotangent, occupancy, neighbours, low, high):
    live = live_of(neighbours)
    for out, rows, edge in ((low, (0, 1), 0), (high, (E - 2, E - 1), E - 1)):
        for i, x in enumerate(rows):
            mask = row_mask(occupancy, live, x)
            out[i] = (features[x, :, 0].astype(F32) * mask).astype(BF16)
            if x == edge:
                out[2] = (cotangent[x, :, 0].astype(F32) * mask).astype(BF16)
                out[3] = mask.astype(BF16)


def faces_y(features, cotangent, occupancy, neighbours, below, above, low, high):
    live = live_of(neighbours)
    for out, first, edge in ((low, 0, 0), (high, E - 2, E - 1)):
        for x in range(E):
            for i in range(2):
                mask = column_mask(occupancy, live, x, first + i)
                out[x + 2, i] = (features[x, first + i, 0].astype(F32) * mask).astype(BF16)
                if first + i == edge:
                    out[x + 2, 2] = (cotangent[x, edge, 0].astype(F32) * mask).astype(BF16)
                    out[x + 2, 3] = mask.astype(BF16)
        for i in range(2):
            out[i, 0:2] = below[i, first : first + 2]
            out[E + 2 + i, 0:2] = above[i, first : first + 2]
        for i in (2, 3):
            out[1, i] = below[i, edge]
            out[E + 2, i] = above[i, edge]
            out[0, i] = jnp.zeros((E, 128), BF16)
            out[E + 3, i] = jnp.zeros((E, 128), BF16)


def spread(store, values, flags, layers):
    rows = lax.broadcasted_iota(jnp.int32, (E, 128), 0)
    down = pltpu.roll(values, 1, 1)
    up = pltpu.roll(values, E - 1, 1)
    for d in layers:
        own = flags[d + 1]
        under = flags[d] if d >= 0 else jnp.zeros((), F32)
        over = flags[d + 2] if d <= 0 else jnp.zeros((), F32)
        store(0, d, down * jnp.where(rows == 0, under, own)[None])
        store(1, d, values * own)
        store(2, d, up * jnp.where(rows == E - 1, over, own)[None])


def for_each_tap(body):
    def step(tap, carry):
        body(tap, tap // 9, (tap // 3) % 3, tap % 3, pl.ds(pl.multiple_of(tap * 128, 128), 128))
        return carry

    lax.fori_loop(0, 27, step, 0)


def gather_own(shifted, patches, first):
    def body(tap, i, j, k, lanes):
        for x in range(E):
            part = shifted(k, first + i + x, pl.ds(first + j, E))
            patches[x * 64 : x * 64 + 64, lanes] = part.reshape(64, 128).astype(BF16)

    return body


def main_kernel(
    features, occupancy, neighbours, first_weight, second_weight, cotangent, below, above, left, right, core,
    keep, send, hidden_out,
    wide, narrow, patches, grad_patches, back_weight, masks, hidden, totals,
):
    live = live_of(neighbours)
    for x in range(E):
        masks[x] = row_mask(occupancy, live, x)

    for p in (-1, 0, 1):
        for q in (-1, 0, 1):
            flags = present(neighbours, p, q)
            count = E if p == 0 else 2
            start = {-1: 0, 0: 2, 1: E + 2}[p]
            columns = {-1: slice(0, 2), 0: slice(2, E + 2), 1: slice(E + 2, E + 4)}[q]

            def wide_row(x, carry, p=p, q=q, flags=flags, start=start, columns=columns):
                if q == -1:
                    values = left[start + x, 0:2].astype(F32)
                elif q == 1:
                    values = right[start + x, 0:2].astype(F32)
                elif p == 0:
                    values = features[x, :, 0].astype(F32) * masks[x]
                else:
                    values = (below if p == -1 else above)[x].astype(F32)

                def store(k, d, tile):
                    wide[k, start + x, columns, d + 1] = tile

                spread(store, values, flags, (-1, 0, 1))
                return carry

            lax.fori_loop(0, count, wide_row, 0)

            count = E if p == 0 else 1
            near = {-1: 0, 0: 1, 1: E + 1}[p]
            columns = {-1: slice(0, 1), 0: slice(1, E + 1), 1: slice(E + 1, E + 2)}[q]

            def narrow_row(x, carry, p=p, q=q, flags=flags, start=near, columns=columns):
                if q == -1:
                    values = left[start + 1 + x, 2:3].astype(F32)
                elif q == 1:
                    values = right[start + 1 + x, 2:3].astype(F32)
                elif p == 0:
                    values = cotangent[x, :, 0].astype(F32) * masks[x]
                else:
                    values = (below if p == -1 else above)[2].astype(F32)

                def store(k, d, tile):
                    narrow[k, start + x, columns] = tile

                spread(store, values, flags, (0,))
                return carry

            lax.fori_loop(0, count, narrow_row, 0)

    def layer_of(p, q):
        flags = present(neighbours, p, q)
        return (1.0 + flags[2] - flags[0]).astype(jnp.int32)

    layer = {(p, q): layer_of(p, q) for p in (-1, 0, 1) for q in (-1, 0, 1)}
    own_rows = gather_own(lambda k, x, ys: wide[k, x, ys, 1], patches, 1)

    def wide_tap(tap, i, j, k, lanes):
        own_rows(tap, i, j, k, lanes)
        edges = (
            wide[k, i, pl.ds(1 + j, E), layer[-1, 0]],
            wide[k, E + 1 + i, pl.ds(1 + j, E), layer[1, 0]],
            wide[k, pl.ds(1 + i, E), j, layer[0, -1]],
            wide[k, pl.ds(1 + i, E), E + 1 + j, layer[0, 1]],
        )
        for n, edge in enumerate(edges):
            patches[512 + 64 * n : 576 + 64 * n, lanes] = edge.reshape(64, 128).astype(BF16)
        corners = [
            wide[k, i + (0 if p < 0 else E + 1), j + (0 if q < 0 else E + 1), layer[p, q]]
            for p in (-1, 1) for q in (-1, 1)
        ]
        patches[768:800, lanes] = jnp.concatenate(corners, axis=0).astype(BF16)

    for_each_tap(wide_tap)

    def narrow_tap(tap, i, j, k, lanes):
        gather_own(lambda k, x, ys: narrow[k, x, ys], grad_patches, 0)(tap, i, j, k, lanes)
        back_weight[:, lanes] = second_weight[26 - tap]

    for_each_tap(narrow_tap)

    pre = jnp.dot(patches[...], first_weight[...], preferred_element_type=F32)
    logistic = jax.nn.sigmoid(pre[:512])
    mask = masks[...].reshape(512, 128)
    own = (pre[:512] * logistic * mask).astype(BF16)
    hidden[1 : E + 1, 1 : E + 1] = own.astype(F32).reshape(E, E, E, 128)
    ring = jax.nn.silu(pre[512:])
    hidden[0, 1 : E + 1] = (ring[0:64].reshape(E, E, 128) * below[3].astype(F32)).astype(BF16).astype(F32)
    hidden[E + 1, 1 : E + 1] = (ring[64:128].reshape(E, E, 128) * above[3].astype(F32)).astype(BF16).astype(F32)
    for x in range(E):
        for y, side, at in ((0, left, 128), (E + 1, right, 192)):
            part = ring[at + 8 * x : at + 8 * x + 8] * side[x + 2, 3].astype(F32)
            hidden[x + 1, y] = part.astype(BF16).astype(F32)
    for n, (x, y) in enumerate(((0, 0), (0, E + 1), (E + 1, 0), (E + 1, E + 1))):
        side = left if y == 0 else right
        part = ring[256 + 8 * n : 264 + 8 * n] * side[x + 1, 3].astype(F32)
        hidden[x, y] = part.astype(BF16).astype(F32)
    hidden_out[...] = hidden[...].astype(BF16)

    slope = logistic * (1.0 + pre[:512] * (1.0 - logistic))
    back = lax.dot_general(
        grad_patches[...], back_weight[...], (((1,), (1,)), ((), ())), preferred_element_type=F32
    )
    grad_pre = (back * slope * mask).astype(BF16)
    first_at = jnp.where(core[0] == 0, 0, 1)
    second = jnp.dot(own.astype(F32).T.astype(BF16), grad_patches[...], preferred_element_type=F32)
    for tap in range(27):
        totals[1 - first_at, tap] = second[:, (26 - tap) * 128 : (27 - tap) * 128]
    first = jnp.dot(grad_pre.astype(F32).T.astype(BF16), patches[0:512], preferred_element_type=F32)
    for tap in range(27):
        totals[first_at, tap] = first[:, tap * 128 : tap * 128 + 128].T

    def out_tap(tap, carry):
        keep[tap] = totals[0, tap]
        send[tap] = totals[1, tap].astype(BF16)
        return carry

    lax.fori_loop(0, 27, out_tap, 0)


def last_kernel(hidden, occupancy, neighbours, second_weight, activations, shifts, patches):
    live = live_of(neighbours)
    for p in (-1, 0, 1):
        for q in (-1, 0, 1):
            flags = present(neighbours, p, q)
            start = {-1: 0, 0: 1, 1: E + 1}[p]
            columns = {-1: slice(0, 1), 0: slice(1, E + 1), 1: slice(E + 1, E + 2)}[q]

            def row(x, carry, flags=flags, start=start, columns=columns):
                def store(k, d, tile):
                    shifts[k, start + x, columns] = tile

                spread(store, hidden[start + x, columns].astype(F32), flags, (0,))
                return carry

            lax.fori_loop(0, E if p == 0 else 1, row, 0)
    for_each_tap(gather_own(lambda k, x, ys: shifts[k, x, ys], patches, 0))
    result = jnp.dot(patches[...], second_weight[...], preferred_element_type=F32)
    for x in range(E):
        part = result[64 * x : 64 * x + 64].reshape(E, E, 128) * row_mask(occupancy, live, x)
        activations[x, :, 0] = part.astype(BF16)


def params():
    return pltpu.CompilerParams(vmem_limit_bytes=LIMIT)


def shape(*dims, dtype=BF16):
    return jax.ShapeDtypeStruct(dims, dtype)


def local_faces_x(features, cotangent, occupancy, neighbours):
    face = shape(4, E, E, 128)
    return pl.pallas_call(
        faces_x, out_shape=(face, face), in_specs=[VMEM, VMEM, SMEM, SMEM], out_specs=(VMEM, VMEM),
        compiler_params=params(), name="faces_x",
    )(features, cotangent, occupancy, neighbours)


def local_faces_y(features, cotangent, occupancy, neighbours, below, above):
    face = shape(E + 4, 4, E, 128)
    return pl.pallas_call(
        faces_y, out_shape=(face, face), in_specs=[VMEM, VMEM, SMEM, SMEM, VMEM, VMEM], out_specs=(VMEM, VMEM),
        compiler_params=params(), name="faces_y",
    )(features, cotangent, occupancy, neighbours, below, above)


def local_main(*operands):
    specs = [VMEM, SMEM, SMEM] + [VMEM] * 7 + [SMEM]
    return pl.pallas_call(
        main_kernel,
        out_shape=(shape(27, 128, 128, dtype=F32), shape(27, 128, 128), shape(E + 2, E + 2, E, 128)),
        in_specs=specs,
        out_specs=(VMEM,) * 3,
        scratch_shapes=[
            pltpu.VMEM((3, E + 4, E + 4, 3, E, 128), F32),
            pltpu.VMEM((3, E + 2, E + 2, E, 128), F32),
            pltpu.VMEM((800, 27 * 128), BF16),
            pltpu.VMEM((512, 27 * 128), BF16),
            pltpu.VMEM((128, 27 * 128), BF16),
            pltpu.VMEM((E, E, E, 128), F32),
            pltpu.VMEM((E + 2, E + 2, E, 128), F32),
            pltpu.VMEM((2, 27, 128, 128), F32),
        ],
        compiler_params=params(),
        cost_estimate=pl.CostEstimate(flops=2 * 2200 * 3456 * 128, bytes_accessed=8000000, transcendentals=100000),
        name="grads",
    )(*operands)


def local_last(hidden, occupancy, neighbours, second_weight):
    return pl.pallas_call(
        last_kernel,
        out_shape=shape(E, E, 1, E, 128),
        in_specs=[VMEM, SMEM, SMEM, VMEM],
        out_specs=VMEM,
        scratch_shapes=[pltpu.VMEM((3, E + 2, E + 2, E, 128), F32), pltpu.VMEM((512, 27 * 128), BF16)],
        compiler_params=params(),
        cost_estimate=pl.CostEstimate(flops=2 * 512 * 3456 * 128, bytes_accessed=2000000, transcendentals=0),
        name="activations",
    )(hidden, occupancy, neighbours, second_weight)


def both_ways(low, high, axis):
    count = lax.axis_size(axis)
    up = [(i, (i + 1) % count) for i in range(count)]
    down = [(j, i) for i, j in up]
    return lax.ppermute(high, axis, up), lax.ppermute(low, axis, down)


def exchange(parts, axes):
    return lax.all_to_all(parts, axes, 0, 0, tiled=True)


def shared(part, count):
    return jnp.broadcast_to(part[None], (count,) + part.shape)


def total_of(keep, send, scale):
    plane_count, along_count = (lax.axis_size(PLANE), lax.axis_size(ALONG))
    got = lax.ppermute(send, "core", SWAP)
    half = (keep + got.astype(F32)).astype(BF16).reshape(-1, 128)
    rows = half.shape[0]
    piece = rows // plane_count
    unit = -(-piece // (16 * along_count)) * 16
    part = exchange(half.reshape(plane_count, piece, 128), PLANE)
    part = jnp.sum(part.astype(F32), axis=0).astype(BF16)
    part = jnp.pad(part, ((0, unit * along_count - piece), (0, 0)))
    part = exchange(part.reshape(along_count, unit, 128), ALONG)
    part = (jnp.sum(part.astype(F32), axis=0) * scale).astype(BF16)
    part = exchange(shared(part, along_count), ALONG).reshape(-1, 128)[:piece]
    half = exchange(shared(part, plane_count), PLANE).reshape(27, 128, 128)
    other = lax.ppermute(half, "core", SWAP)
    first = lax.axis_index("core") == 0
    return jnp.where(first, half, other), jnp.where(first, other, half)


def local(features, occupancy, neighbours, first_weight, second_weight, cotangent):
    low, high = local_faces_x(features, cotangent, occupancy, neighbours)
    below, above = both_ways(low, high, GX)
    low, high = local_faces_y(features, cotangent, occupancy, neighbours, below, above)
    left, right = both_ways(low, high, GY)
    core = lax.axis_index("core").astype(jnp.int32).reshape(1)
    keep, send, hidden = local_main(
        features, occupancy, neighbours, first_weight.reshape(-1, 128), second_weight, cotangent,
        below, above, left, right, core,
    )
    activations = local_last(hidden, occupancy, neighbours, second_weight.reshape(-1, 128))
    scale = 1.0 / math.sqrt(E**3 * lax.axis_size(GX) * lax.axis_size(GY))
    first_grad, second_grad = total_of(keep, send, scale)
    return activations, first_grad, second_grad


def solution(mesh):
    fine = Mesh(mesh.devices.reshape(2, 16, 2, 2, 4), GX + GY)
    field = P(GX, GY, None, None, None)
    in_specs = (field, P(GX, GY, None), P(GX, GY, None, None), P(), P(), field)
    return jax.shard_map(local, mesh=fine, in_specs=in_specs, out_specs=(field, P(), P()), check_vma=False)
```

time: 627 us -> 137 us (0.22)
  waiting for transfers between devices: 492 us -> 4.52 us
  blocking collectives: 0 us -> 69.2 us
  between operations: 49.6 us -> 0.8 us
  matrix products: 15.7 us -> 0 us
  Pallas kernels: 0 us -> 15.6 us
  local copies, waits for them, and re-layouts: 19.8 us -> 8.21 us
  other arithmetic: 9.65 us -> 1.71 us
    psum x1 -> x0, waiting for transfers between devices: 492 us -> none  [local(): lax.psum((first_total, second_total), ('gx', 'gy'))]
    all_to_all x0 -> x4, blocking collectives: none -> 69.2 us  [exchange(): return lax.all_to_all(parts, axes, 0, 0, tiled=True)]
    dot_general x4 -> x0, matrix products: 15.7 us -> none  [the longest x2 10.9 us: outer_sum(): lax.dot_general(patches.reshape(-1, patches.shape[-1]), grads.reshape(-1,...]
    pallas_call x0 -> x4, Pallas kernels: none -> 15.6 us  [the longest x1 9.2 us: local_main(): pl.pallas_call(main_kernel, out_shape=(shape(27, 128, 128, dtype=F32), sh...]
    unnamed x135 -> x21, local copies, waits for them, and re-layouts: 14.9 us -> 8.07 us
    ppermute x12 -> x6, starting transfers between devices: 38.1 us -> 36 us  [the longest x4 19.6 us: both_ways(): return (lax.ppermute(high, axis, up), lax.ppermute(low, axis, down))]
  transfers between devices with their start and end apart: 13 -> 6, of which waited for: 2 -> 4; matrix products, arithmetic and copies ran while one was open for 5% -> 0% of each run, Pallas kernels for 0% -> 3%
where the time goes in v2:
time: 137 us; the launch traced here: 136 us
  blocking collectives  69.2 us (51%)
  starting transfers between devices  36 us (26%)
  Pallas kernels  15.6 us (11%)
  local copies, waits for them, and re-layouts  8.21 us (6%)
  waiting for transfers between devices  4.52 us (3%)
  other arithmetic  1.71 us (1%)
    all_to_all x4, blocking collectives, exchange(): return lax.all_to_all(parts, axes, 0, 0, tiled=True)  69.2 us
    ppermute x4, starting transfers between devices, both_ways(): return (lax.ppermute(high, axis, up), lax.ppermute(low, axis, down))  19.6 us
    pallas_call x1, Pallas kernels, local_main(): pl.pallas_call(main_kernel, out_shape=(shape(27, 128, 128, dtype=F32), sh...  9.2 us
    ppermute x1, starting transfers between devices, total_of(): got = lax.ppermute(send, 'core', SWAP)  8.54 us
    unnamed x21, local copies, waits for them, and re-layouts  8.07 us
    ppermute x1, starting transfers between devices, total_of(): other = lax.ppermute(half, 'core', SWAP)  7.81 us
    pallas_call x1, Pallas kernels, local_last(): pl.pallas_call(last_kernel, out_shape=shape(E, E, 1, E, 128), in_specs=[V...  4.18 us
  transfers between devices with their start and end apart: 6, of which 4 were waited for; matrix products, arithmetic and copies ran while one was open for 0% of the time, Pallas kernels for 3%

profile of v2, /device:TPU:1, one launch (start us, length us, event | category | flops | bytes accessed | tf_op | source)
XLA Modules:
  0.0 136.0 jit_solution(257404357664488075)
XLA Ops:
  1.4 0.9 copy-done
  2.3 0.9 copy-done.2
  3.9 1.1 faces_x.1
  5.0 4.9 %collective-permute-start = (bf16[4,8,8,128]{3,2,1,0:T(8,128)(2,1)S(1)}, bf16[4,8,8,128]{3,2,1,0:T(8,128)(2,1)S(1)}, u32[]{:S(2)}, u32[]{:S(2)}) collective-permute-start(bf16[4,8,8,128]{3,2,1,0:T(8,128)(2,1)S(1)} %get-tuple-element.10), channel_id=1, source_target_pairs={{0,8},{8,16},{16,24},{24,32},{32,40},{40,48},{48,56},{56,64},{64,7... | collective-permute-start | bytes 196616 | tf_op jit(solution)/shard_map/ppermute | solution.py:318
  10.0 5.8 %collective-permute-start.1 = (bf16[4,8,8,128]{3,2,1,0:T(8,128)(2,1)S(1)}, bf16[4,8,8,128]{3,2,1,0:T(8,128)(2,1)S(1)}, u32[]{:S(2)}, u32[]{:S(2)}) collective-permute-start(bf16[4,8,8,128]{3,2,1,0:T(8,128)(2,1)S(1)} %get-tuple-element.11), channel_id=1, source_target_pairs={{8,0},{16,8},{24,16},{32,24},{40,32},{48,40},{56,48},{64,56},{72,6... | collective-permute-start | bytes 196616 | tf_op jit(solution)/shard_map/ppermute | solution.py:318
  15.8 0.9 collective-permute-done.1.above
  16.6 1.1 faces_y.1
  17.7 2.1 %collective-permute-start.2 = (bf16[12,4,8,128]{3,2,1,0:T(8,128)(2,1)S(1)}, bf16[12,4,8,128]{3,2,1,0:T(8,128)(2,1)S(1)}, u32[]{:S(2)}, u32[]{:S(2)}) collective-permute-start(bf16[12,4,8,128]{3,2,1,0:T(8,128)(2,1)S(1)} %get-tuple-element.12), channel_id=1, source_target_pairs={{0,1},{1,2},{2,3},{3,4},{4,5},{5,6},{6,7},{7,0},{8,9},{9,10},{10,1... | collective-permute-start | bytes 294920 | tf_op jit(solution)/shard_map/ppermute | solution.py:318
  19.9 6.8 %collective-permute-start.3 = (bf16[12,4,8,128]{3,2,1,0:T(8,128)(2,1)S(1)}, bf16[12,4,8,128]{3,2,1,0:T(8,128)(2,1)S(1)}, u32[]{:S(2)}, u32[]{:S(2)}) collective-permute-start(bf16[12,4,8,128]{3,2,1,0:T(8,128)(2,1)S(1)} %get-tuple-element.13), channel_id=1, source_target_pairs={{1,0},{2,1},{3,2},{4,3},{5,4},{6,5},{7,6},{0,7},{9,8},{10,9},{11,1... | collective-permute-start | bytes 294920 | tf_op jit(solution)/shard_map/ppermute | solution.py:318
  26.7 1.6 %collective-permute-done.3.right = bf16[12,4,8,128]{3,2,1,0:T(8,128)(2,1)S(1)} collective-permute-done((bf16[12,4,8,128]{3,2,1,0:T(8,128)(2,1)S(1)}, bf16[12,4,8,128]{3,2,1,0:T(8,128)(2,1)S(1)}, u32[]{:S(2)}, u32[]{:S(2)}) %collective-permute-start.3) | collective-permute-done | bytes 98336 | tf_op jit(solution)/shard_map/ppermute | solution.py:318
  28.3 0.9 copy-done.1
  29.2 0.9 copy-done.3
  30.7 1.2 copy-done.7
  31.9 1.2 copy-done.8
  33.1 9.2 %grads.1 = (f32[27,128,128]{2,1,0:T(8,128)S(1)}, bf16[27,128,128]{2,1,0:T(8,128)(2,1)S(1)}, bf16[10,10,8,128]{3,2,1,0:T(8,128)(2,1)S(1)}) custom-call(bf16[8,8,1,8,128]{4,3,2,1,0:T(8,128)(2,1)S(1)} %copy-done.1, s32[8,8,1]{2,1,0:T(8,128)S(1)} %copy.15.occupancy, s32[1,1,1,27]{3,2,1,0:T(1,128)S(1)} %copy-done.5, bf16[3456,128]{1,0:T(8,128)(2,1)S(1)} %bitcast.7, ...), custom_call_target="tpu_custom_call" | custom-call | flops 1946419200 | bytes 8000000 | tf_op jit(solution)/shard_map/grads/pallas_call | solution.py:280
  42.3 8.5 %collective-permute-start.4 = (bf16[27,128,128]{2,1,0:T(8,128)(2,1)S(1)}, bf16[27,128,128]{2,1,0:T(8,128)(2,1)S(1)}, u32[]{:S(2)}, u32[]{:S(2)}) collective-permute-start(bf16[27,128,128]{2,1,0:T(8,128)(2,1)S(1)} %get-tuple-element.16), channel_id=1, source_target_pairs={{0,8},{8,0},{1,9},{9,1},{2,10},{10,2},{3,11},{11,3},{4,12},{12,4},... | collective-permute-start | bytes 2654216 | tf_op jit(solution)/shard_map/ppermute | solution.py:331
  50.8 2.0 %collective-permute-done.4 = bf16[27,128,128]{2,1,0:T(8,128)(2,1)S(1)} collective-permute-done((bf16[27,128,128]{2,1,0:T(8,128)(2,1)S(1)}, bf16[27,128,128]{2,1,0:T(8,128)(2,1)S(1)}, u32[]{:S(2)}, u32[]{:S(2)}) %collective-permute-start.4) | collective-permute-done | bytes 884768 | tf_op jit(solution)/shard_map/ppermute | solution.py:331
  53.1 20.9 %all_to_all.20 = bf16[16,216,128]{2,1,0:T(8,128)(2,1)S(1)} all-to-all(bf16[16,216,128]{2,1,0:T(8,128)(2,1)S(1)} %bitcast.9), channel_id=1, replica_groups=mesh['x_lo'=2,'z'=16,'core'=2,'x_hi'=2,'y'=4] {'x_lo','x_hi','y'}, dimensions={0} | all-to-all | bytes 1769472 | tf_op jit(solution)/shard_map/all_to_all | solution.py:322
  74.2 20.1 %all_to_all.21 = bf16[16,16,128]{2,1,0:T(8,128)(2,1)S(1)} all-to-all(bf16[16,16,128]{2,1,0:T(8,128)(2,1)S(1)} %bitcast.12), channel_id=1, replica_groups=mesh['x_lo'=2,'z'=16,'core'=2,'x_hi'=2,'y'=4] {'z'}, dimensions={0} | all-to-all | bytes 131072 | tf_op jit(solution)/shard_map/all_to_all | solution.py:322
  94.4 14.4 %all_to_all.22 = bf16[16,16,128]{2,1,0:T(8,128)(2,1)S(1)} all-to-all(bf16[16,16,128]{2,1,0:T(8,128)(2,1)S(1)} %broadcast_in_dim.4), channel_id=1, replica_groups=mesh['x_lo'=2,'z'=16,'core'=2,'x_hi'=2,'y'=4] {'z'}, dimensions={0} | all-to-all | bytes 131072 | tf_op jit(solution)/shard_map/all_to_all | solution.py:322
  108.9 13.8 %all_to_all.23 = bf16[16,216,128]{2,1,0:T(8,128)(2,1)S(1)} all-to-all(bf16[16,216,128]{2,1,0:T(8,128)(2,1)S(1)} %broadcast_in_dim.5), channel_id=1, replica_groups=mesh['x_lo'=2,'z'=16,'core'=2,'x_hi'=2,'y'=4] {'x_lo','x_hi','y'}, dimensions={0} | all-to-all | bytes 1769472 | tf_op jit(solution)/shard_map/all_to_all | solution.py:322
  122.7 7.8 %collective-permute-start.5 = (bf16[27,128,128]{2,1,0:T(8,128)(2,1)S(1)}, bf16[27,128,128]{2,1,0:T(8,128)(2,1)S(1)}, u32[]{:S(2)}, u32[]{:S(2)}) collective-permute-start(bf16[27,128,128]{2,1,0:T(8,128)(2,1)S(1)} %bitcast.10), channel_id=1, source_target_pairs={{0,8},{8,0},{1,9},{9,1},{2,10},{10,2},{3,11},{11,3},{4,12},{12,4},... | collective-permute-start | bytes 2654216 | tf_op jit(solution)/shard_map/ppermute | solution.py:343
  130.5 4.2 %activations.1 = bf16[8,8,1,8,128]{4,3,2,1,0:T(8,128)(2,1)} custom-call(bf16[10,10,8,128]{3,2,1,0:T(8,128)(2,1)S(1)} %get-tuple-element.14.hidden, s32[8,8,1]{2,1,0:T(8,128)S(1)} %copy.15.occupancy, s32[1,1,1,27]{3,2,1,0:T(1,128)S(1)} %copy-done.6, bf16[3456,128]{1,0:T(8,128)(2,1)S(1)} %bitcast.8), custom_call_target="tpu_custom_call" | custom-call | flops 452984832 | bytes 2000000 | tf_op jit(solution)/shard_map/activations/pallas_call | solution.py:302
  134.7 1.3 broadcast_select_fusion
  (26 shorter events, 2.7 us)
Async XLA Ops:
  1.4 0.9 copy-start
  2.3 0.9 copy-start.2
  3.2 0.7 copy-start.4
  5.0 10.7 %collective-permute-start = (bf16[4,8,8,128]{3,2,1,0:T(8,128)(2,1)S(1)}, bf16[4,8,8,128]{3,2,1,0:T(8,128)(2,1)S(1)}, u32[]{:S(2)}, u32[]{:S(2)}) collective-permute-start(bf16[4,8,8,128]{3,2,1,0:T(8,128)(2,1)S(1)} %get-tuple-element.10), channel_id=1, source_target_pairs={{0,8},{8,16},{16,24},{24,32},{32,40},{40,48},{48,56},{56,64},{64,7... | collective-permute-start | bytes 196616 | tf_op jit(solution)/shard_map/ppermute | solution.py:318
  10.0 6.7 %collective-permute-start.1 = (bf16[4,8,8,128]{3,2,1,0:T(8,128)(2,1)S(1)}, bf16[4,8,8,128]{3,2,1,0:T(8,128)(2,1)S(1)}, u32[]{:S(2)}, u32[]{:S(2)}) collective-permute-start(bf16[4,8,8,128]{3,2,1,0:T(8,128)(2,1)S(1)} %get-tuple-element.11), channel_id=1, source_target_pairs={{8,0},{16,8},{24,16},{32,24},{40,32},{48,40},{56,48},{64,56},{72,6... | collective-permute-start | bytes 196616 | tf_op jit(solution)/shard_map/ppermute | solution.py:318
  17.7 9.0 %collective-permute-start.2 = (bf16[12,4,8,128]{3,2,1,0:T(8,128)(2,1)S(1)}, bf16[12,4,8,128]{3,2,1,0:T(8,128)(2,1)S(1)}, u32[]{:S(2)}, u32[]{:S(2)}) collective-permute-start(bf16[12,4,8,128]{3,2,1,0:T(8,128)(2,1)S(1)} %get-tuple-element.12), channel_id=1, source_target_pairs={{0,1},{1,2},{2,3},{3,4},{4,5},{5,6},{6,7},{7,0},{8,9},{9,10},{10,1... | collective-permute-start | bytes 294920 | tf_op jit(solution)/shard_map/ppermute | solution.py:318
  19.9 8.4 %collective-permute-start.3 = (bf16[12,4,8,128]{3,2,1,0:T(8,128)(2,1)S(1)}, bf16[12,4,8,128]{3,2,1,0:T(8,128)(2,1)S(1)}, u32[]{:S(2)}, u32[]{:S(2)}) collective-permute-start(bf16[12,4,8,128]{3,2,1,0:T(8,128)(2,1)S(1)} %get-tuple-element.13), channel_id=1, source_target_pairs={{1,0},{2,1},{3,2},{4,3},{5,4},{6,5},{7,6},{0,7},{9,8},{10,9},{11,1... | collective-permute-start | bytes 294920 | tf_op jit(solution)/shard_map/ppermute | solution.py:318
  28.3 0.9 copy-start.1
  29.2 0.9 copy-start.3
  30.1 0.7 copy-start.5
  30.7 1.2 copy-start.7
  31.9 1.2 copy-start.8
  42.3 10.6 %collective-permute-start.4 = (bf16[27,128,128]{2,1,0:T(8,128)(2,1)S(1)}, bf16[27,128,128]{2,1,0:T(8,128)(2,1)S(1)}, u32[]{:S(2)}, u32[]{:S(2)}) collective-permute-start(bf16[27,128,128]{2,1,0:T(8,128)(2,1)S(1)} %get-tuple-element.16), channel_id=1, source_target_pairs={{0,8},{8,0},{1,9},{9,1},{2,10},{10,2},{3,11},{11,3},{4,12},{12,4},... | collective-permute-start | bytes 2654216 | tf_op jit(solution)/shard_map/ppermute | solution.py:331
  74.2 56.4 %copy-start.6 = (s32[1,1,1,27]{3,2,1,0:T(1,128)S(1)}, s32[1,1,1,27]{3,2,1,0:T(1,128)}, u32[]{:S(2)}) copy-start(s32[1,1,1,27]{3,2,1,0:T(1,128)} %neighbours.7) | copy-start | bytes 328
  74.2 56.4 %copy-start.9 = (bf16[27,128,128]{2,1,0:T(8,128)(2,1)S(1)}, bf16[27,128,128]{2,1,0:T(8,128)(2,1)}, u32[]{:S(2)}) copy-start(bf16[27,128,128]{2,1,0:T(8,128)(2,1)} %second_weight.1) | copy-start | bytes 2654212
  122.7 12.0 %collective-permute-start.5 = (bf16[27,128,128]{2,1,0:T(8,128)(2,1)S(1)}, bf16[27,128,128]{2,1,0:T(8,128)(2,1)S(1)}, u32[]{:S(2)}, u32[]{:S(2)}) collective-permute-start(bf16[27,128,128]{2,1,0:T(8,128)(2,1)S(1)} %bitcast.10), channel_id=1, source_target_pairs={{0,8},{8,0},{1,9},{9,1},{2,10},{10,2},{3,11},{11,3},{4,12},{12,4},... | collective-permute-start | bytes 2654216 | tf_op jit(solution)/shard_map/ppermute | solution.py:343

commit v3 on v0

v3 whole, which is shorter than its diff:
```python
import functools
import math

import jax
import jax.numpy as jnp
from jax import lax
from jax.experimental import pallas as pl
from jax.experimental.pallas import tpu as pltpu
from jax.sharding import Mesh
from jax.sharding import PartitionSpec as P

GX = ("x_lo", "z_hi", "z_lo", "core")
GY = ("x_hi", "y")
NEAR = ("x_lo", "z_lo", "x_hi", "y")
FAR = ("z_hi",)
SWAP = [(0, 1), (1, 0)]
F32 = jnp.float32
BF16 = jnp.bfloat16
E = 8
LIMIT = 48 * 1024 * 1024
VMEM = pl.BlockSpec(memory_space=pltpu.VMEM)
SMEM = pl.BlockSpec(memory_space=pltpu.SMEM)
HBM = pl.BlockSpec(memory_space=pltpu.HBM)


def bits_of(occupied):
    layers = lax.broadcasted_iota(jnp.int32, (E, 128), 0)
    return (jnp.right_shift(occupied, layers) & 1).astype(F32)


def row_mask(occupied, x):
    return jnp.stack([bits_of(jnp.full((E, 128), occupied(x, y), jnp.int32)) for y in range(E)])


def present(neighbours, p, q):
    base = 9 * (p + 1) + 3 * (q + 1)
    return [jnp.where(neighbours[0, base + r] >= 0, 1.0, 0.0).astype(F32) for r in range(3)]


def live_of(neighbours):
    return jnp.where(neighbours[0, 13] >= 0, 1, 0)


def is_even(axis):
    return lax.rem(lax.axis_index(axis), 2) == 0


def start_all(copies):
    for copy in copies:
        copy.start()
    return copies


def wait_all(copies):
    for copy in copies:
        copy.wait()


def faces_x(
    features, cotangent, occupancy, neighbours, masked, graded, masks, out_a, out_b, own, grads, occupied, table, sems
):
    copies = start_all([
        pltpu.make_async_copy(occupancy, occupied, sems.at[0]),
        pltpu.make_async_copy(neighbours, table, sems.at[1]),
        pltpu.make_async_copy(features, own, sems.at[2]),
        pltpu.make_async_copy(cotangent, grads, sems.at[3]),
    ])
    even = is_even("core")
    wait_all(copies[:2])
    live = live_of(table)
    for x in range(E):
        masks[x] = row_mask(lambda x, y: occupied[x, y] * live, x)
    wait_all(copies[2:])
    for x in range(E):
        masked[x] = (own[x].astype(F32) * masks[x]).astype(BF16)
        graded[x] = (grads[x].astype(F32) * masks[x]).astype(BF16)
    rows = lax.broadcasted_iota(jnp.int32, (E, 128), 0)
    for out, high in ((out_a, jnp.where(even, 1, 0)), (out_b, jnp.where(even, 0, 1))):
        edge = (E - 1) * high
        for i in range(2):
            out[E * i : E * i + E] = masked[(E - 2) * high + i]
        out[16:24] = graded[edge]
        values = jnp.zeros((E, 128), jnp.int32)
        for y in range(E):
            values = jnp.where(rows == y, occupied[edge, y] * live, values)
        out[24] = values.astype(F32).astype(BF16)


def faces_y(masked, graded, masks, from_a, from_b, out_a, out_b):
    even_x = is_even("core")
    even = is_even("y")
    rows = lax.broadcasted_iota(jnp.int32, (E, 128), 0)
    weights = jnp.left_shift(jnp.ones((E, 128), jnp.int32), rows).astype(F32)
    zero = jnp.zeros((E, 128), BF16)
    for out, high in ((out_a, jnp.where(even, 1, 0)), (out_b, jnp.where(even, 0, 1))):
        first, edge = ((E - 2) * high, (E - 1) * high)
        for i in range(2):
            for x in range(E):
                out[12 * i + 2 + x] = masked[x, first + i]
                if i == 0:
                    out[26 + x] = graded[x, edge]
            for x in range(2):
                low_a, low_b = (from_a[E * x + first + i], from_b[E * x + first + i])
                out[12 * i + x] = jnp.where(even_x, low_b, low_a)
                out[12 * i + E + 2 + x] = jnp.where(even_x, low_a, low_b)
        at_a, at_b = (from_a[16 + edge], from_b[16 + edge])
        out[24] = zero
        out[35] = zero
        out[25] = jnp.where(even_x, at_b, at_a)
        out[34] = jnp.where(even_x, at_a, at_b)
        values = jnp.zeros((E, 128), F32)
        for x in range(E):
            values = jnp.where(rows == x, jnp.sum(masks[x, edge] * weights, axis=0, keepdims=True), values)
        out[36] = values.astype(BF16)
        in_a, in_b = (from_a[24].astype(F32), from_b[24].astype(F32))
        corner_a = jnp.sum(jnp.where(rows == edge, in_a, 0.0), axis=0, keepdims=True)
        corner_b = jnp.sum(jnp.where(rows == edge, in_b, 0.0), axis=0, keepdims=True)
        low, above = (jnp.where(even_x, corner_b, corner_a), jnp.where(even_x, corner_a, corner_b))
        out[37] = jnp.where(rows == 0, low, jnp.where(rows == 1, above, 0.0)).astype(BF16)


def spread(store, values, flags, layers):
    rows = lax.broadcasted_iota(jnp.int32, (E, 128), 0)
    down = pltpu.roll(values, 1, 1)
    up = pltpu.roll(values, E - 1, 1)
    for d in layers:
        own = flags[d + 1]
        under = flags[d] if d >= 0 else jnp.zeros((), F32)
        over = flags[d + 2] if d <= 0 else jnp.zeros((), F32)
        store(0, d, down * jnp.where(rows == 0, under, own)[None])
        store(1, d, values * own)
        store(2, d, up * jnp.where(rows == E - 1, over, own)[None])


def spread_window(shifts, neighbours, value_of, width, layers):
    for p in (-1, 0, 1):
        for q in (-1, 0, 1):
            flags = present(neighbours, p, q)
            start = {-1: 0, 0: width, 1: E + width}[p]
            columns = {-1: slice(0, width), 0: slice(width, E + width), 1: slice(E + width, E + 2 * width)}[q]

            def row(x, carry, p=p, q=q, flags=flags, start=start, columns=columns):
                def store(k, d, tile):
                    if len(layers) == 1:
                        shifts[k, start + x, columns] = tile
                    else:
                        shifts[k, start + x, columns, d + 1] = tile

                spread(store, value_of(p, q, x, start + x), flags, layers)
                return carry

            lax.fori_loop(0, E if p == 0 else width, row, 0)


def for_each_tap(body):
    def step(tap, carry):
        body(tap, tap // 9, (tap // 3) % 3, tap % 3, pl.ds(pl.multiple_of(tap * 128, 128), 128))
        return carry

    lax.fori_loop(0, 27, step, 0)


def gather_own(shifts, patches, i, j, k, lanes):
    for x in range(E):
        part = shifts[k, i + x, pl.ds(j, E)]
        patches[x * 64 : x * 64 + 64, lanes] = part.reshape(64, 128).astype(BF16)


def main_kernel(
    masked, graded, masks, neighbours, first_weight, second_weight, x_a, x_b, y_a, y_b,
    keep, send, hidden_out,
    first_taps, second_taps, shifts, grad_shifts, patches, grad_patches, back_weight, table, sems,
):
    copies = start_all([
        pltpu.make_async_copy(neighbours, table, sems.at[0]),
        pltpu.make_async_copy(second_weight, second_taps, sems.at[1]),
        pltpu.make_async_copy(first_weight, first_taps, sems.at[2]),
    ])
    even_x = is_even("core")
    even_y = is_even("y")
    wait_all(copies[:1])

    def masked_at(p, q, x, at):
        if q == -1:
            return jnp.where(even_y, y_b[12 + at + 1], y_a[12 + at + 1]).astype(F32)[None]
        if q == 1:
            return jnp.where(even_y, y_a[at + 1], y_b[at + 1]).astype(F32)[None]
        if p == -1:
            return jnp.where(even_x, x_b[E : 2 * E], x_a[E : 2 * E]).astype(F32)
        if p == 1:
            return jnp.where(even_x, x_a[0:E], x_b[0:E]).astype(F32)
        return masked[x].astype(F32)

    def grad_at(p, q, x, at):
        if q == -1:
            return jnp.where(even_y, y_b[24 + at + 1], y_a[24 + at + 1]).astype(F32)[None]
        if q == 1:
            return jnp.where(even_y, y_a[24 + at + 1], y_b[24 + at + 1]).astype(F32)[None]
        if p == -1:
            return jnp.where(even_x, x_b[16:24], x_a[16:24]).astype(F32)
        if p == 1:
            return jnp.where(even_x, x_a[16:24], x_b[16:24]).astype(F32)
        return graded[x].astype(F32)

    spread_window(shifts, table, masked_at, 1, (0,))
    spread_window(grad_shifts, table, grad_at, 1, (0,))
    wait_all(copies[1:])

    def fill(tap, i, j, k, lanes):
        gather_own(shifts, patches, i, j, k, lanes)
        gather_own(grad_shifts, grad_patches, i, j, k, lanes)
        back_weight[:, lanes] = second_taps[26 - tap]

    for_each_tap(fill)

    pre = jnp.dot(patches[...], first_taps[...], preferred_element_type=F32)
    logistic = jax.nn.sigmoid(pre)
    mask = masks[...].reshape(512, 128)
    hidden = (pre * logistic * mask).astype(BF16)
    hidden_out[...] = hidden.reshape(E, E, E, 128)
    back = lax.dot_general(
        grad_patches[...], back_weight[...], (((1,), (1,)), ((), ())), preferred_element_type=F32
    )
    grad_pre = (back * (logistic * (1.0 + pre * (1.0 - logistic))) * mask).astype(BF16)
    hidden_turned = hidden.astype(F32).T.astype(BF16)
    grad_turned = grad_pre.astype(F32).T.astype(BF16)
    second = jnp.dot(hidden_turned, grad_patches[...], preferred_element_type=F32)
    first = jnp.dot(grad_turned, patches[...], preferred_element_type=F32)
    for tap in range(27):
        first_tap = first[:, tap * 128 : tap * 128 + 128].T
        second_tap = second[:, (26 - tap) * 128 : (27 - tap) * 128]
        keep[tap] = jnp.where(even_x, first_tap, second_tap)
        send[tap] = jnp.where(even_x, second_tap, first_tap).astype(BF16)
    keep[27] = jnp.zeros((128, 128), F32)
    send[27] = jnp.zeros((128, 128), BF16)


def last_kernel(
    masked, masks, neighbours, first_weight, second_weight, x_a, x_b, y_a, y_b, hidden_own,
    activations,
    first_taps, second_taps, wide, hidden, shifts, ring_patches, patches, table, sems,
):
    copies = start_all([
        pltpu.make_async_copy(neighbours, table, sems.at[0]),
        pltpu.make_async_copy(first_weight, first_taps, sems.at[1]),
        pltpu.make_async_copy(second_weight, second_taps, sems.at[2]),
    ])
    even_x = is_even("core")
    even_y = is_even("y")

    def below(tiles):
        return jnp.where(even_x, x_b[tiles], x_a[tiles]).astype(F32)

    def above(tiles):
        return jnp.where(even_x, x_a[tiles], x_b[tiles]).astype(F32)

    def left(tiles):
        return jnp.where(even_y, y_b[tiles], y_a[tiles]).astype(F32)

    def right(tiles):
        return jnp.where(even_y, y_a[tiles], y_b[tiles]).astype(F32)

    def mask_of(tile, row):
        return bits_of(jnp.broadcast_to(tile[row : row + 1], (E, 128)).astype(jnp.int32))

    wait_all(copies[:1])

    def masked_at(p, q, x, at):
        if q != 0:
            side = left if q == -1 else right
            return jnp.stack([side(at), side(12 + at)])
        if p != 0:
            return (below if p == -1 else above)(pl.ds(E * x, E))
        return masked[x].astype(F32)

    spread_window(wide, table, masked_at, 2, (-1, 0, 1))

    def layer_of(p, q):
        flags = present(table, p, q)
        return (1.0 + flags[2] - flags[0]).astype(jnp.int32)

    layer = {(p, q): layer_of(p, q) for p in (-1, 0, 1) for q in (-1, 0, 1)}

    def ring_tap(tap, i, j, k, lanes):
        edges = (
            wide[k, i, pl.ds(1 + j, E), layer[-1, 0]],
            wide[k, E + 1 + i, pl.ds(1 + j, E), layer[1, 0]],
            wide[k, pl.ds(1 + i, E), j, layer[0, -1]],
            wide[k, pl.ds(1 + i, E), E + 1 + j, layer[0, 1]],
        )
        for n, edge in enumerate(edges):
            ring_patches[64 * n : 64 * n + 64, lanes] = edge.reshape(64, 128).astype(BF16)
        corners = [
            wide[k, i + (0 if p < 0 else E + 1), j + (0 if q < 0 else E + 1), layer[p, q]]
            for p in (-1, 1) for q in (-1, 1)
        ]
        ring_patches[256:288, lanes] = jnp.concatenate(corners, axis=0).astype(BF16)

    for_each_tap(ring_tap)
    wait_all(copies[1:])

    ring = jax.nn.silu(jnp.dot(ring_patches[...], first_taps[...], preferred_element_type=F32))
    low, high = (below(24), above(24))
    sides = [(side(36), side(37)) for side in (left, right)]
    for y in range(E):
        hidden[0, y + 1] = (ring[8 * y : 8 * y + 8] * mask_of(low, y)).astype(BF16).astype(F32)
        hidden[E + 1, y + 1] = (ring[64 + 8 * y : 72 + 8 * y] * mask_of(high, y)).astype(BF16).astype(F32)
    for x in range(E):
        hidden[x + 1, 1 : E + 1] = hidden_own[x].astype(F32)
        for n, y in enumerate((0, E + 1)):
            part = ring[128 + 64 * n + 8 * x : 136 + 64 * n + 8 * x] * mask_of(sides[n][0], x)
            hidden[x + 1, y] = part.astype(BF16).astype(F32)
    for m, x in enumerate((0, E + 1)):
        for n, y in enumerate((0, E + 1)):
            at = 256 + 16 * m + 8 * n
            hidden[x, y] = (ring[at : at + 8] * mask_of(sides[n][1], m)).astype(BF16).astype(F32)

    def hidden_at(p, q, x, at):
        columns = {-1: slice(0, 1), 0: slice(1, E + 1), 1: slice(E + 1, E + 2)}[q]
        return hidden[at, columns]

    spread_window(shifts, table, hidden_at, 1, (0,))
    for_each_tap(lambda tap, i, j, k, lanes: gather_own(shifts, patches, i, j, k, lanes))
    result = jnp.dot(patches[...], second_taps[...], preferred_element_type=F32)
    for x in range(E):
        part = result[64 * x : 64 * x + 64].reshape(E, E, 128) * masks[x]
        activations[x] = part.astype(BF16)


def params():
    return pltpu.CompilerParams(vmem_limit_bytes=LIMIT)


def shape(*dims, dtype=BF16):
    return jax.ShapeDtypeStruct(dims, dtype)


def vmem(*dims, dtype=BF16):
    return pltpu.VMEM(dims, dtype)


def held(array):
    return pltpu.with_memory_space_constraint(array, pltpu.HBM)


def local_faces_x(features, cotangent, occupancy, neighbours):
    face, field = (shape(25, E, 128), shape(E, E, E, 128))
    return pl.pallas_call(
        faces_x,
        out_shape=(field, field, shape(E, E, E, 128, dtype=F32), face, face),
        in_specs=[HBM] * 4,
        out_specs=(VMEM,) * 5,
        scratch_shapes=[
            vmem(E, E, E, 128), vmem(E, E, E, 128), pltpu.SMEM((E, E), jnp.int32), pltpu.SMEM((1, 27), jnp.int32),
            pltpu.SemaphoreType.DMA((4,)),
        ],
        compiler_params=params(), name="faces_x",
    )(*map(held, (features, cotangent, occupancy, neighbours)))


def local_faces_y(*operands):
    face = shape(38, E, 128)
    return pl.pallas_call(
        faces_y, out_shape=(face, face), in_specs=[VMEM] * 5, out_specs=(VMEM, VMEM),
        compiler_params=params(), name="faces_y",
    )(*operands)


def local_main(*operands):
    return pl.pallas_call(
        main_kernel,
        out_shape=(shape(28, 128, 128, dtype=F32), shape(28, 128, 128), shape(E, E, E, 128)),
        in_specs=[VMEM] * 3 + [HBM] * 3 + [VMEM] * 4,
        out_specs=(VMEM,) * 3,
        scratch_shapes=[
            vmem(27 * 128, 128), vmem(27, 128, 128),
            vmem(3, E + 2, E + 2, E, 128, dtype=F32), vmem(3, E + 2, E + 2, E, 128, dtype=F32),
            vmem(512, 27 * 128), vmem(512, 27 * 128), vmem(128, 27 * 128),
            pltpu.SMEM((1, 27), jnp.int32), pltpu.SemaphoreType.DMA((3,)),
        ],
        compiler_params=params(),
        cost_estimate=pl.CostEstimate(flops=8 * 512 * 3456 * 128, bytes_accessed=8000000, transcendentals=100000),
        name="grads",
    )(*operands)


def local_last(*operands):
    return pl.pallas_call(
        last_kernel,
        out_shape=shape(E, E, E, 128),
        in_specs=[VMEM] * 2 + [HBM] * 3 + [VMEM] * 5,
        out_specs=VMEM,
        scratch_shapes=[
            vmem(27 * 128, 128), vmem(27 * 128, 128),
            vmem(3, E + 4, E + 4, 3, E, 128, dtype=F32),
            vmem(E + 2, E + 2, E, 128, dtype=F32),
            vmem(3, E + 2, E + 2, E, 128, dtype=F32),
            vmem(288, 27 * 128), vmem(512, 27 * 128),
            pltpu.SMEM((1, 27), jnp.int32), pltpu.SemaphoreType.DMA((3,)),
        ],
        compiler_params=params(),
        cost_estimate=pl.CostEstimate(flops=4 * 800 * 3456 * 128, bytes_accessed=2000000, transcendentals=40000),
        name="activations",
    )(*operands)


def paired(out_a, out_b, axis):
    count = lax.axis_size(axis)
    pairs_a = [(i, i ^ 1) for i in range(count)]
    pairs_b = [(i, ((i - 1) ^ 1) + 1) for i in range(1, count - 1)]
    from_b = lax.ppermute(out_b, axis, pairs_b)
    return lax.ppermute(out_a, axis, pairs_a), from_b


def exchange(parts, axes):
    return lax.all_to_all(parts, axes, 0, 0, tiled=True)


def shared(part, count):
    return jnp.broadcast_to(part[None], (count,) + part.shape)


def summed(parts):
    return jnp.sum(parts.astype(F32), axis=0)


def local(features, occupancy, neighbours, first_weight, second_weight, cotangent):
    features, cotangent = (array.reshape(E, E, E, 128) for array in (features, cotangent))
    occupancy, neighbours = (occupancy.reshape(E, E), neighbours.reshape(1, 27))
    first_taps, second_taps = (weight.reshape(27 * 128, 128) for weight in (first_weight, second_weight))
    masked, graded, masks, *out = local_faces_x(features, cotangent, occupancy, neighbours)
    x_a, x_b = paired(*out, GX)
    y_a, y_b = paired(*local_faces_y(masked, graded, masks, x_a, x_b), GY)
    faces = (x_a, x_b, y_a, y_b)
    keep, send, hidden = local_main(
        masked, graded, masks, *map(held, (neighbours, first_taps, second_weight)), *faces
    )
    activations = local_last(
        masked, masks, *map(held, (neighbours, first_taps, second_taps)), *faces, hidden
    )
    scale = 1.0 / math.sqrt(E**3 * lax.axis_size(GX) * lax.axis_size(GY))
    near, far = (lax.axis_size(NEAR), lax.axis_size(FAR))
    got = lax.ppermute(send, "core", SWAP)
    half = (keep + got.astype(F32)).astype(BF16)
    part = summed(exchange(half.reshape(near, -1, 128), NEAR)).astype(BF16)
    part = summed(exchange(shared(part, far), FAR))
    part, activations = lax.optimization_barrier((part, activations))
    part = (part * scale).astype(BF16)
    half = exchange(shared(part, near), NEAR).reshape(28, 128, 128)
    other = lax.ppermute(half, "core", SWAP)
    first = lax.axis_index("core") == 0
    first_grad = jnp.where(first, half, other)[:27]
    second_grad = jnp.where(first, other, half)[:27]
    return activations.reshape(E, E, 1, E, 128), first_grad, second_grad


def solution(mesh):
    fine = Mesh(mesh.devices.reshape(2, 8, 2, 2, 2, 4), GX + GY)
    field = P(GX, GY, None, None, None)
    in_specs = (field, P(GX, GY, None), P(GX, GY, None, None), P(), P(), field)
    return jax.shard_map(local, mesh=fine, in_specs=in_specs, out_specs=(field, P(), P()), check_vma=False)
```

time: 627 us -> 114 us (0.18)
  waiting for transfers between devices: 492 us -> 19.2 us
  between operations: 49.6 us -> 0.75 us
  blocking collectives: 0 us -> 45.9 us
  local copies, waits for them, and re-layouts: 19.8 us -> 0.84 us
  matrix products: 15.7 us -> 0 us
  Pallas kernels: 0 us -> 14.2 us
  other arithmetic: 9.65 us -> 1.77 us
  starting transfers between devices: 38.1 us -> 30.7 us
    psum x1 -> x0, waiting for transfers between devices: 492 us -> none  [local(): lax.psum((first_total, second_total), ('gx', 'gy'))]
    all_to_all x0 -> x2, blocking collectives: none -> 45.9 us  [exchange(): return lax.all_to_all(parts, axes, 0, 0, tiled=True)]
    dot_general x4 -> x0, matrix products: 15.7 us -> none  [the longest x2 10.9 us: outer_sum(): lax.dot_general(patches.reshape(-1, patches.shape[-1]), grads.reshape(-1,...]
    ppermute x12 -> x6, starting transfers between devices: 38.1 us -> 22.5 us  [the longest x2 10.7 us: paired(): return (lax.ppermute(out_a, axis, pairs_a), from_b)]
    unnamed x135 -> x0, local copies, waits for them, and re-layouts: 14.9 us -> none
    pallas_call x0 -> x4, Pallas kernels: none -> 14.2 us  [the longest x1 6.92 us: local_last(): pl.pallas_call(last_kernel, out_shape=shape(E, E, E, 128), in_specs=[VMEM...]
    ppermute x12 -> x6, waiting for transfers between devices: 0.56 us -> 10.5 us  [the longest x2 3.49 us: paired(): from_b = lax.ppermute(out_b, axis, pairs_b)]
    all_to_all x0 -> x1, waiting for transfers between devices: none -> 8.69 us  [exchange(): return lax.all_to_all(parts, axes, 0, 0, tiled=True)]
  transfers between devices with their start and end apart: 13 -> 7, of which waited for: 2 -> 5; matrix products, arithmetic and copies ran while one was open for 5% -> 0% of each run, Pallas kernels for 0% -> 6%
where the time goes in v3:
time: 114 us; the launch traced here: 113 us
  blocking collectives  45.9 us (40%)
  starting transfers between devices  30.7 us (27%)
  waiting for transfers between devices  19.2 us (17%)
  Pallas kernels  14.2 us (12%)
  other arithmetic  1.77 us (2%)
    all_to_all x2, blocking collectives, exchange(): return lax.all_to_all(parts, axes, 0, 0, tiled=True)  45.9 us
    ppermute x2, starting transfers between devices, paired(): return (lax.ppermute(out_a, axis, pairs_a), from_b)  10.7 us
    all_to_all x1, waiting for transfers between devices, exchange(): return lax.all_to_all(parts, axes, 0, 0, tiled=True)  8.69 us
    all_to_all x1, starting transfers between devices, exchange(): return lax.all_to_all(parts, axes, 0, 0, tiled=True)  8.2 us
    ppermute x1, starting transfers between devices, local(): other = lax.ppermute(half, 'core', SWAP)  7.25 us
    pallas_call x1, Pallas kernels, local_last(): pl.pallas_call(last_kernel, out_shape=shape(E, E, E, 128), in_specs=[VMEM...  6.92 us
    pallas_call x1, Pallas kernels, local_main(): pl.pallas_call(main_kernel, out_shape=(shape(28, 128, 128, dtype=F32), sh...  6.21 us
    ppermute x2, waiting for transfers between devices, paired(): from_b = lax.ppermute(out_b, axis, pairs_b)  3.49 us
  transfers between devices with their start and end apart: 7, of which 5 were waited for; matrix products, arithmetic and copies ran while one was open for 0% of the time, Pallas kernels for 6%

profile of v3, /device:TPU:1, one launch (start us, length us, event | category | flops | bytes accessed | tf_op | source)
XLA Modules:
  0.0 113.4 jit_solution(3665493367243455967)
XLA Ops:
  0.6 1.1 faces_x.1
  1.7 8.8 %collective-permute-start = (bf16[25,8,128]{2,1,0:T(8,128)(2,1)S(1)}, bf16[25,8,128]{2,1,0:T(8,128)(2,1)S(1)}, u32[]{:S(2)}, u32[]{:S(2)}) collective-permute-start(bf16[25,8,128]{2,1,0:T(8,128)(2,1)S(1)} %get-tuple-element.18), channel_id=1, source_target_pairs={{0,8},{8,0},{16,24},{24,16},{32,40},{40,32},{48,56},{56,48},{64,72... | collective-permute-start | bytes 153608 | tf_op jit(solution)/shard_map/ppermute | solution.py:412
  10.5 1.9 %collective-permute-start.1 = (bf16[25,8,128]{2,1,0:T(8,128)(2,1)S(1)}, bf16[25,8,128]{2,1,0:T(8,128)(2,1)S(1)}, u32[]{:S(2)}, u32[]{:S(2)}) collective-permute-start(bf16[25,8,128]{2,1,0:T(8,128)(2,1)S(1)} %get-tuple-element.19), channel_id=1, source_target_pairs={{8,16},{16,8},{24,32},{32,24},{40,48},{48,40},{56,64},{64,56},{72,... | collective-permute-start | bytes 153608 | tf_op jit(solution)/shard_map/ppermute | solution.py:411
  12.4 3.5 %collective-permute-done.1.from_b.x_b = bf16[25,8,128]{2,1,0:T(8,128)(2,1)S(1)} collective-permute-done((bf16[25,8,128]{2,1,0:T(8,128)(2,1)S(1)}, bf16[25,8,128]{2,1,0:T(8,128)(2,1)S(1)}, u32[]{:S(2)}, u32[]{:S(2)}) %collective-permute-start.1) | collective-permute-done | bytes 51232 | tf_op jit(solution)/shard_map/ppermute | solution.py:411
  15.9 0.1 faces_y.1
  16.0 1.9 %collective-permute-start.2 = (bf16[38,8,128]{2,1,0:T(8,128)(2,1)S(1)}, bf16[38,8,128]{2,1,0:T(8,128)(2,1)S(1)}, u32[]{:S(2)}, u32[]{:S(2)}) collective-permute-start(bf16[38,8,128]{2,1,0:T(8,128)(2,1)S(1)} %get-tuple-element.20), channel_id=1, source_target_pairs={{0,1},{1,0},{2,3},{3,2},{4,5},{5,4},{6,7},{7,6},{8,9},{9,8},{10,11... | collective-permute-start | bytes 233480 | tf_op jit(solution)/shard_map/ppermute | solution.py:412
  17.9 0.7 collective-permute-start.3
  18.6 2.5 %collective-permute-done.2.y_a = bf16[38,8,128]{2,1,0:T(8,128)(2,1)S(1)} collective-permute-done((bf16[38,8,128]{2,1,0:T(8,128)(2,1)S(1)}, bf16[38,8,128]{2,1,0:T(8,128)(2,1)S(1)}, u32[]{:S(2)}, u32[]{:S(2)}) %collective-permute-start.2) | collective-permute-done | bytes 77856 | tf_op jit(solution)/shard_map/ppermute | solution.py:412
  21.1 0.0 collective-permute-done.3.y_b
  21.1 6.2 %grads.1 = (f32[28,128,128]{2,1,0:T(8,128)S(1)}, bf16[28,128,128]{2,1,0:T(8,128)(2,1)S(1)}, bf16[8,8,8,128]{3,2,1,0:T(8,128)(2,1)S(1)}) custom-call(bf16[8,8,8,128]{3,2,1,0:T(8,128)(2,1)S(1)} %get-tuple-element.15.masked, bf16[8,8,8,128]{3,2,1,0:T(8,128)(2,1)S(1)} %get-tuple-element.16.graded, f32[8,8,8,128]{3,2,1,0:T(8,128)S(1)} %get-tuple-element.17.masks, ...), custom_call_target="tpu_custom_call" | custom-call | flops 1811939328 | bytes 8000000 | tf_op jit(solution)/shard_map/grads/pallas_call | solution.py:370
  27.3 1.9 %collective-permute-start.4 = (bf16[28,128,128]{2,1,0:T(8,128)(2,1)S(1)}, bf16[28,128,128]{2,1,0:T(8,128)(2,1)S(1)}, u32[]{:S(2)}, u32[]{:S(2)}) collective-permute-start(bf16[28,128,128]{2,1,0:T(8,128)(2,1)S(1)} %get-tuple-element.23), channel_id=1, source_target_pairs={{0,8},{8,0},{1,9},{9,1},{2,10},{10,2},{3,11},{11,3},{4,12},{12,4},... | collective-permute-start | bytes 2752520 | tf_op jit(solution)/shard_map/ppermute | solution.py:443
  29.3 2.4 %collective-permute-done.4 = bf16[28,128,128]{2,1,0:T(8,128)(2,1)S(1)} collective-permute-done((bf16[28,128,128]{2,1,0:T(8,128)(2,1)S(1)}, bf16[28,128,128]{2,1,0:T(8,128)(2,1)S(1)}, u32[]{:S(2)}, u32[]{:S(2)}) %collective-permute-start.4) | collective-permute-done | bytes 917536 | tf_op jit(solution)/shard_map/ppermute | solution.py:443
  31.7 0.3 add_convert_fusion
  32.0 29.0 %all_to_all.15 = bf16[32,112,128]{2,1,0:T(8,128)(2,1)S(1)} all-to-all(bf16[32,112,128]{2,1,0:T(8,128)(2,1)S(1)} %bitcast.11), channel_id=1, replica_groups=mesh['x_lo'=2,'z_hi'=8,'z_lo'=2,'core'=2,'x_hi'=2,'y'=4] {'x_lo','z_lo',..., dimensions={0} | all-to-all | bytes 1835008 | tf_op jit(solution)/shard_map/all_to_all | solution.py:416
  61.0 0.1 reduce_sum.21
  61.1 0.7 broadcast_in_dim.4
  61.8 8.2 %all-to-all-start.1 = ((bf16[8,112,128]{2,1,0:T(8,128)(2,1)}), bf16[8,112,128]{2,1,0:T(8,128)(2,1)S(1)}, u32[]{:S(2)}, u32[]{:S(2)}) async-start(bf16[8,112,128]{2,1,0:T(8,128)(2,1)} %broadcast_in_dim.4), calls=%async_computation.1 | async-start | bytes 458752 | tf_op jit(solution)/shard_map/all_to_all | solution.py:416
  70.0 6.9 %activations.1 = bf16[8,8,8,128]{3,2,1,0:T(8,128)(2,1)} custom-call(bf16[8,8,8,128]{3,2,1,0:T(8,128)(2,1)S(1)} %get-tuple-element.15.masked, f32[8,8,8,128]{3,2,1,0:T(8,128)S(1)} %get-tuple-element.17.masks, s32[1,27]{1,0:T(1,128)} %bitcast.19, bf16[3456,128]{1,0:T(8,128)(2,1)} %bitcast.21, bf16[3456,128]{1,0:T(8,128)(2,1)} %bitcast.22, ...), custom_call_target="tpu_custom_call" | custom-call | flops 1415577600 | bytes 2000000 | tf_op jit(solution)/shard_map/activations/pallas_call | solution.py:388
  77.0 8.7 %all-to-all-done.1 = bf16[8,112,128]{2,1,0:T(8,128)(2,1)S(1)} async-done(((bf16[8,112,128]{2,1,0:T(8,128)(2,1)}), bf16[8,112,128]{2,1,0:T(8,128)(2,1)S(1)}, u32[]{:S(2)}, u32[]{:S(2)}) %all-to-all-start.1) | async-done | bytes 229408 | tf_op jit(solution)/shard_map/all_to_all | solution.py:416
  85.7 0.1 broadcast_in_dim.5
  85.8 16.9 %all_to_all.16 = bf16[32,112,128]{2,1,0:T(8,128)(2,1)S(1)} all-to-all(bf16[32,112,128]{2,1,0:T(8,128)(2,1)S(1)} %broadcast_in_dim.5), channel_id=1, replica_groups=mesh['x_lo'=2,'z_hi'=8,'z_lo'=2,'core'=2,'x_hi'=2,'y'=4] {'x_lo','z_lo',..., dimensions={0} | all-to-all | bytes 1835008 | tf_op jit(solution)/shard_map/all_to_all | solution.py:416
  102.8 7.2 %collective-permute-start.5 = (bf16[28,128,128]{2,1,0:T(8,128)(2,1)S(1)}, bf16[28,128,128]{2,1,0:T(8,128)(2,1)S(1)}, u32[]{:S(2)}, u32[]{:S(2)}) collective-permute-start(bf16[28,128,128]{2,1,0:T(8,128)(2,1)S(1)} %bitcast.12), channel_id=1, source_target_pairs={{0,8},{8,0},{1,9},{9,1},{2,10},{10,2},{3,11},{11,3},{4,12},{12,4},... | collective-permute-start | bytes 2752520 | tf_op jit(solution)/shard_map/ppermute | solution.py:450
  110.0 2.1 %collective-permute-done.5 = bf16[28,128,128]{2,1,0:T(8,128)(2,1)S(1)} collective-permute-done((bf16[28,128,128]{2,1,0:T(8,128)(2,1)S(1)}, bf16[28,128,128]{2,1,0:T(8,128)(2,1)S(1)}, u32[]{:S(2)}, u32[]{:S(2)}) %collective-permute-start.5) | collective-permute-done | bytes 917536 | tf_op jit(solution)/shard_map/ppermute | solution.py:450
  112.1 1.3 %broadcast_select_fusion = (bf16[27,128,128]{2,1,0:T(8,128)(2,1)}, bf16[27,128,128]{2,1,0:T(8,128)(2,1)}) fusion(pred[]{:T(512)S(6)} %eq.3, bf16[28,128,128]{2,1,0:T(8,128)(2,1)S(1)} %collective-permute-done.5, bf16[28,128,128]{2,1,0:T(8,128)(2,1)S(1)} %bitcast.13), kind=kLoop, calls=%fused_computation.1 | loop fusion | flops 884736 | bytes 3538945 | tf_op jit(solution)/shard_map/jit(_where)/select_n | solution.py:453
  (3 shorter events, 0.0 us)
Async XLA Ops:
  1.7 10.7 %collective-permute-start = (bf16[25,8,128]{2,1,0:T(8,128)(2,1)S(1)}, bf16[25,8,128]{2,1,0:T(8,128)(2,1)S(1)}, u32[]{:S(2)}, u32[]{:S(2)}) collective-permute-start(bf16[25,8,128]{2,1,0:T(8,128)(2,1)S(1)} %get-tuple-element.18), channel_id=1, source_target_pairs={{0,8},{8,0},{16,24},{24,16},{32,40},{40,32},{48,56},{56,48},{64,72... | collective-permute-start | bytes 153608 | tf_op jit(solution)/shard_map/ppermute | solution.py:412
  10.5 5.4 %collective-permute-start.1 = (bf16[25,8,128]{2,1,0:T(8,128)(2,1)S(1)}, bf16[25,8,128]{2,1,0:T(8,128)(2,1)S(1)}, u32[]{:S(2)}, u32[]{:S(2)}) collective-permute-start(bf16[25,8,128]{2,1,0:T(8,128)(2,1)S(1)} %get-tuple-element.19), channel_id=1, source_target_pairs={{8,16},{16,8},{24,32},{32,24},{40,48},{48,40},{56,64},{64,56},{72,... | collective-permute-start | bytes 153608 | tf_op jit(solution)/shard_map/ppermute | solution.py:411
  16.0 5.1 %collective-permute-start.2 = (bf16[38,8,128]{2,1,0:T(8,128)(2,1)S(1)}, bf16[38,8,128]{2,1,0:T(8,128)(2,1)S(1)}, u32[]{:S(2)}, u32[]{:S(2)}) collective-permute-start(bf16[38,8,128]{2,1,0:T(8,128)(2,1)S(1)} %get-tuple-element.20), channel_id=1, source_target_pairs={{0,1},{1,0},{2,3},{3,2},{4,5},{5,4},{6,7},{7,6},{8,9},{9,8},{10,11... | collective-permute-start | bytes 233480 | tf_op jit(solution)/shard_map/ppermute | solution.py:412
  17.9 3.2 %collective-permute-start.3 = (bf16[38,8,128]{2,1,0:T(8,128)(2,1)S(1)}, bf16[38,8,128]{2,1,0:T(8,128)(2,1)S(1)}, u32[]{:S(2)}, u32[]{:S(2)}) collective-permute-start(bf16[38,8,128]{2,1,0:T(8,128)(2,1)S(1)} %get-tuple-element.21), channel_id=1, source_target_pairs={{1,2},{2,1},{3,4},{4,3},{5,6},{6,5},{9,10},{10,9},{11,12},{12,11},... | collective-permute-start | bytes 233480 | tf_op jit(solution)/shard_map/ppermute | solution.py:411
  27.3 4.4 %collective-permute-start.4 = (bf16[28,128,128]{2,1,0:T(8,128)(2,1)S(1)}, bf16[28,128,128]{2,1,0:T(8,128)(2,1)S(1)}, u32[]{:S(2)}, u32[]{:S(2)}) collective-permute-start(bf16[28,128,128]{2,1,0:T(8,128)(2,1)S(1)} %get-tuple-element.23), channel_id=1, source_target_pairs={{0,8},{8,0},{1,9},{9,1},{2,10},{10,2},{3,11},{11,3},{4,12},{12,4},... | collective-permute-start | bytes 2752520 | tf_op jit(solution)/shard_map/ppermute | solution.py:443
  61.8 23.8 %all-to-all-start.1 = ((bf16[8,112,128]{2,1,0:T(8,128)(2,1)}), bf16[8,112,128]{2,1,0:T(8,128)(2,1)S(1)}, u32[]{:S(2)}, u32[]{:S(2)}) async-start(bf16[8,112,128]{2,1,0:T(8,128)(2,1)} %broadcast_in_dim.4), calls=%async_computation.1 | async-start | bytes 458752 | tf_op jit(solution)/shard_map/all_to_all | solution.py:416
  102.8 9.3 %collective-permute-start.5 = (bf16[28,128,128]{2,1,0:T(8,128)(2,1)S(1)}, bf16[28,128,128]{2,1,0:T(8,128)(2,1)S(1)}, u32[]{:S(2)}, u32[]{:S(2)}) collective-permute-start(bf16[28,128,128]{2,1,0:T(8,128)(2,1)S(1)} %bitcast.12), channel_id=1, source_target_pairs={{0,8},{8,0},{1,9},{9,1},{2,10},{10,2},{3,11},{11,3},{4,12},{12,4},... | collective-permute-start | bytes 2752520 | tf_op jit(solution)/shard_map/ppermute | solution.py:450

commit v4 on v3

--- a/solution.py
+++ b/solution.py
@@ -17,7 +17,7 @@
 F32 = jnp.float32
 BF16 = jnp.bfloat16
 E = 8
-LIMIT = 48 * 1024 * 1024
+LIMIT = 30 * 1024 * 1024
 VMEM = pl.BlockSpec(memory_space=pltpu.VMEM)
 SMEM = pl.BlockSpec(memory_space=pltpu.SMEM)
 HBM = pl.BlockSpec(memory_space=pltpu.HBM)
@@ -57,7 +57,7 @@
 
 
 def faces_x(
-    features, cotangent, occupancy, neighbours, masked, graded, masks, out_a, out_b, own, grads, occupied, table, sems
+    features, cotangent, occupancy, neighbours, masked, graded, masks, out_b, out_a, own, grads, occupied, table, sems
 ):
     copies = start_all([
         pltpu.make_async_copy(occupancy, occupied, sems.at[0]),
@@ -86,7 +86,7 @@
         out[24] = values.astype(F32).astype(BF16)
 
 
-def faces_y(masked, graded, masks, from_a, from_b, out_a, out_b):
+def faces_y(masked, graded, masks, from_b, from_a, out_b, out_a):
     even_x = is_even("core")
     even = is_even("y")
     rows = lax.broadcasted_iota(jnp.int32, (E, 128), 0)
@@ -166,19 +166,31 @@
         patches[x * 64 : x * 64 + 64, lanes] = part.reshape(64, 128).astype(BF16)
 
 
+def weights_kernel(first_weight, second_weight, first_taps, back_weight, second_taps, sems):
+    copies = start_all([
+        pltpu.make_async_copy(second_weight, second_taps, sems.at[0]),
+        pltpu.make_async_copy(first_weight, first_taps, sems.at[1]),
+    ])
+    copies[0].wait()
+
+    def turn(tap, i, j, k, lanes):
+        back_weight[:, lanes] = second_taps[26 - tap]
+
+    for_each_tap(turn)
+    copies[1].wait()
+
+
 def main_kernel(
-    masked, graded, masks, neighbours, first_weight, second_weight, x_a, x_b, y_a, y_b,
-    keep, send, hidden_out,
-    first_taps, second_taps, shifts, grad_shifts, patches, grad_patches, back_weight, table, sems,
+    masked, graded, masks, neighbours, first_taps, back_weight, x_b, x_a, y_b, y_a,
+    send, hidden_out, factors, patches,
+    shifts, grad_shifts, raw, table, sems,
 ):
     copies = start_all([
         pltpu.make_async_copy(neighbours, table, sems.at[0]),
-        pltpu.make_async_copy(second_weight, second_taps, sems.at[1]),
-        pltpu.make_async_copy(first_weight, first_taps, sems.at[2]),
     ])
     even_x = is_even("core")
     even_y = is_even("y")
-    wait_all(copies[:1])
+    wait_all(copies)
 
     def masked_at(p, q, x, at):
         if q == -1:
@@ -204,39 +216,49 @@
 
     spread_window(shifts, table, masked_at, 1, (0,))
     spread_window(grad_shifts, table, grad_at, 1, (0,))
-    wait_all(copies[1:])
 
     def fill(tap, i, j, k, lanes):
-        gather_own(shifts, patches, i, j, k, lanes)
-        gather_own(grad_shifts, grad_patches, i, j, k, lanes)
-        back_weight[:, lanes] = second_taps[26 - tap]
+        gather_own(shifts, patches.at[0], i, j, k, lanes)
+        gather_own(grad_shifts, patches.at[1], i, j, k, lanes)
 
     for_each_tap(fill)
 
-    pre = jnp.dot(patches[...], first_taps[...], preferred_element_type=F32)
+    pre = jnp.dot(patches[0], first_taps[...], preferred_element_type=F32)
     logistic = jax.nn.sigmoid(pre)
     mask = masks[...].reshape(512, 128)
     hidden = (pre * logistic * mask).astype(BF16)
     hidden_out[...] = hidden.reshape(E, E, E, 128)
     back = lax.dot_general(
-        grad_patches[...], back_weight[...], (((1,), (1,)), ((), ())), preferred_element_type=F32
+        patches[1], back_weight[...], (((1,), (1,)), ((), ())), preferred_element_type=F32
     )
     grad_pre = (back * (logistic * (1.0 + pre * (1.0 - logistic))) * mask).astype(BF16)
-    hidden_turned = hidden.astype(F32).T.astype(BF16)
-    grad_turned = grad_pre.astype(F32).T.astype(BF16)
-    second = jnp.dot(hidden_turned, grad_patches[...], preferred_element_type=F32)
-    first = jnp.dot(grad_turned, patches[...], preferred_element_type=F32)
-    for tap in range(27):
-        first_tap = first[:, tap * 128 : tap * 128 + 128].T
-        second_tap = second[:, (26 - tap) * 128 : (27 - tap) * 128]
-        keep[tap] = jnp.where(even_x, first_tap, second_tap)
-        send[tap] = jnp.where(even_x, second_tap, first_tap).astype(BF16)
-    keep[27] = jnp.zeros((128, 128), F32)
-    send[27] = jnp.zeros((128, 128), BF16)
+    factors[0] = grad_pre.astype(F32).T.astype(BF16)
+    factors[1] = hidden.astype(F32).T.astype(BF16)
+    taps_of(factors, patches, jnp.where(even_x, 1, 0), send, raw)
+
+
+def keep_kernel(factors, patches, keep, raw):
+    taps_of(factors, patches, jnp.where(is_even("core"), 0, 1), keep, raw)
+
+
+def taps_of(factors, patches, which, out, raw):
+    raw[...] = jnp.dot(factors[which], patches[which], preferred_element_type=F32)
+
+    @pl.when(which == 0)
+    def _():
+        for tap in range(27):
+            out[tap] = raw[:, tap * 128 : tap * 128 + 128].T.astype(out.dtype)
+
+    @pl.when(which == 1)
+    def _():
+        for tap in range(27):
+            out[tap] = raw[:, (26 - tap) * 128 : (27 - tap) * 128].astype(out.dtype)
+
+    out[27] = jnp.zeros((128, 128), out.dtype)
 
 
 def last_kernel(
-    masked, masks, neighbours, first_weight, second_weight, x_a, x_b, y_a, y_b, hidden_own,
+    masked, masks, neighbours, first_weight, second_weight, x_b, x_a, y_b, y_a, hidden_own,
     activations,
     first_taps, second_taps, wide, hidden, shifts, ring_patches, patches, table, sems,
 ):
@@ -366,22 +388,83 @@
     )(*operands)
 
 
+def local_weights(first_weight, second_weight):
+    return pl.pallas_call(
+        weights_kernel,
+        out_shape=(shape(27 * 128, 128), shape(128, 27 * 128)),
+        in_specs=[HBM] * 2,
+        out_specs=(VMEM,) * 2,
+        scratch_shapes=[vmem(27, 128, 128), pltpu.SemaphoreType.DMA((2,))],
+        compiler_params=params(),
+        cost_estimate=pl.CostEstimate(flops=0, bytes_accessed=8000000, transcendentals=0),
+        name="weights",
+    )(held(first_weight), held(second_weight))
+
+
 def local_main(*operands):
     return pl.pallas_call(
         main_kernel,
-        out_shape=(shape(28, 128, 128, dtype=F32), shape(28, 128, 128), shape(E, E, E, 128)),
-        in_specs=[VMEM] * 3 + [HBM] * 3 + [VMEM] * 4,
-        out_specs=(VMEM,) * 3,
+        out_shape=(
+            shape(28, 128, 128), shape(E, E, E, 128), shape(2, 128, 512), shape(2, 512, 27 * 128)
+        ),
+        in_specs=[VMEM] * 3 + [HBM] + [VMEM] * 6,
+        out_specs=(VMEM,) * 4,
         scratch_shapes=[
-            vmem(27 * 128, 128), vmem(27, 128, 128),
             vmem(3, E + 2, E + 2, E, 128, dtype=F32), vmem(3, E + 2, E + 2, E, 128, dtype=F32),
-            vmem(512, 27 * 128), vmem(512, 27 * 128), vmem(128, 27 * 128),
-            pltpu.SMEM((1, 27), jnp.int32), pltpu.SemaphoreType.DMA((3,)),
+            vmem(128, 27 * 128, dtype=F32),
+            pltpu.SMEM((1, 27), jnp.int32), pltpu.SemaphoreType.DMA((1,)),
         ],
         compiler_params=params(),
         cost_estimate=pl.CostEstimate(flops=8 * 512 * 3456 * 128, bytes_accessed=8000000, transcendentals=100000),
         name="grads",
     )(*operands)
+
+
+def local_keep(factors, patches):
+    return pl.pallas_call(
+        keep_kernel,
+        out_shape=shape(28, 128, 128, dtype=F32),
+        in_specs=[VMEM] * 2,
+        out_specs=VMEM,
+        scratch_shapes=[vmem(128, 27 * 128, dtype=F32)],
+        compiler_params=params(),
+        cost_estimate=pl.CostEstimate(flops=8 * 512 * 3456 * 128, bytes_accessed=6000000, transcendentals=0),
+        name="kept",
+    )(*(pltpu.with_memory_space_constraint(array, pltpu.VMEM) for array in (factors, patches)))
+
+
+def place_kernel(own, source, *refs):
+    first, second, sem = refs[-3:]
+
+    def place(out):
+        copy = pltpu.make_async_copy(source.at[pl.ds(0, 27)], out, sem)
+        copy.start()
+        copy.wait()
+
+    even = is_even("core")
+
+    @pl.when(even if own else jnp.logical_not(even))
+    def _():
+        place(first)
+
+    @pl.when(jnp.logical_not(even) if own else even)
+    def _():
+        place(second)
+
+
+def local_place(source, outs=()):
+    gradient = shape(27, 128, 128)
+    return pl.pallas_call(
+        functools.partial(place_kernel, not outs),
+        out_shape=(gradient, gradient),
+        in_specs=[pl.BlockSpec(memory_space=pl.ANY)] + [HBM] * len(outs),
+        out_specs=(HBM, HBM),
+        scratch_shapes=[pltpu.SemaphoreType.DMA(())],
+        input_output_aliases={1: 0, 2: 1} if outs else {},
+        compiler_params=params(),
+        cost_estimate=pl.CostEstimate(flops=0, bytes_accessed=4000000, transcendentals=0),
+        name="place_other" if outs else "place_own",
+    )(source, *outs)
 
 
 def local_last(*operands):
@@ -404,12 +487,11 @@
     )(*operands)
 
 
-def paired(out_a, out_b, axis):
+def paired(out_b, out_a, axis):
     count = lax.axis_size(axis)
     pairs_a = [(i, i ^ 1) for i in range(count)]
     pairs_b = [(i, ((i - 1) ^ 1) + 1) for i in range(1, count - 1)]
-    from_b = lax.ppermute(out_b, axis, pairs_b)
-    return lax.ppermute(out_a, axis, pairs_a), from_b
+    return lax.ppermute(out_b, axis, pairs_b), lax.ppermute(out_a, axis, pairs_a)
 
 
 def exchange(parts, axes):
@@ -429,11 +511,11 @@
     occupancy, neighbours = (occupancy.reshape(E, E), neighbours.reshape(1, 27))
     first_taps, second_taps = (weight.reshape(27 * 128, 128) for weight in (first_weight, second_weight))
     masked, graded, masks, *out = local_faces_x(features, cotangent, occupancy, neighbours)
-    x_a, x_b = paired(*out, GX)
-    y_a, y_b = paired(*local_faces_y(masked, graded, masks, x_a, x_b), GY)
-    faces = (x_a, x_b, y_a, y_b)
-    keep, send, hidden = local_main(
-        masked, graded, masks, *map(held, (neighbours, first_taps, second_weight)), *faces
+    x_b, x_a = paired(*out, GX)
+    y_b, y_a = paired(*local_faces_y(masked, graded, masks, x_b, x_a), GY)
+    faces = (x_b, x_a, y_b, y_a)
+    send, hidden, factors, patches = local_main(
+        masked, graded, masks, held(neighbours), *local_weights(first_taps, second_weight), *faces
     )
     activations = local_last(
         masked, masks, *map(held, (neighbours, first_taps, second_taps)), *faces, hidden
@@ -441,6 +523,7 @@
     scale = 1.0 / math.sqrt(E**3 * lax.axis_size(GX) * lax.axis_size(GY))
     near, far = (lax.axis_size(NEAR), lax.axis_size(FAR))
     got = lax.ppermute(send, "core", SWAP)
+    keep = local_keep(factors, patches)
     half = (keep + got.astype(F32)).astype(BF16)
     part = summed(exchange(half.reshape(near, -1, 128), NEAR)).astype(BF16)
     part = summed(exchange(shared(part, far), FAR))
@@ -448,9 +531,7 @@
     part = (part * scale).astype(BF16)
     half = exchange(shared(part, near), NEAR).reshape(28, 128, 128)
     other = lax.ppermute(half, "core", SWAP)
-    first = lax.axis_index("core") == 0
-    first_grad = jnp.where(first, half, other)[:27]
-    second_grad = jnp.where(first, other, half)[:27]
+    first_grad, second_grad = local_place(other, local_place(half))
     return activations.reshape(E, E, 1, E, 128), first_grad, second_grad
 
 

time: 114 us -> 109 us (0.956)
  waiting for transfers between devices: 19.2 us -> 12.7 us
  Pallas kernels: 14.2 us -> 17.8 us
  other arithmetic: 1.77 us -> 0.43 us
    ppermute x4, waiting for transfers between devices: 6.04 us -> 1.61 us  [the longest x2 1.6 us: paired(): lax.ppermute(out_a, axis, pairs_a)]
    pallas_call x1 -> x5, Pallas kernels: 6.21 us -> 9.78 us  [the longest x1 5.65 us: local_main(): pl.pallas_call(main_kernel, out_shape=(shape(28, 128, 128), shape(E, E, E...]
    select_n x1 -> x0, other arithmetic: 1.32 us -> none  [local(): second_grad = jnp.where(first, other, half)[:27]]
    ppermute x1, waiting for transfers between devices: 2.44 us -> 1.29 us  [local(): got = lax.ppermute(send, 'core', SWAP)]
  transfers between devices with their start and end apart: 7 -> 7, of which waited for: 5 -> 5; matrix products, arithmetic and copies ran while one was open for 0% -> 0% of each run, Pallas kernels for 6% -> 9%
where the time goes in v4:
time: 109 us
  blocking collectives  45 us (41%)
  starting transfers between devices  31.1 us (29%)
  Pallas kernels  17.8 us (16%)
  waiting for transfers between devices  12.7 us (12%)
    all_to_all x2, blocking collectives, exchange(): return lax.all_to_all(parts, axes, 0, 0, tiled=True)  45 us
    all_to_all x1, waiting for transfers between devices, exchange(): return lax.all_to_all(parts, axes, 0, 0, tiled=True)  8.69 us
    ppermute x2, starting transfers between devices, paired(): lax.ppermute(out_a, axis, pairs_a)  8 us
    all_to_all x1, starting transfers between devices, exchange(): return lax.all_to_all(parts, axes, 0, 0, tiled=True)  7.51 us
    ppermute x1, starting transfers between devices, local(): other = lax.ppermute(half, 'core', SWAP)  7.25 us
    pallas_call x1, Pallas kernels, local_last(): pl.pallas_call(last_kernel, out_shape=shape(E, E, E, 128), in_specs=[VMEM...  6.91 us
    pallas_call x1, Pallas kernels, local_main(): pl.pallas_call(main_kernel, out_shape=(shape(28, 128, 128), shape(E, E, E...  5.65 us
    ppermute x2, starting transfers between devices, paired(): lax.ppermute(out_b, axis, pairs_b)  5.6 us
  transfers between devices with their start and end apart: 7, of which 5 were waited for; matrix products, arithmetic and copies ran while one was open for 0% of the time, Pallas kernels for 9%

profile of v4, /device:TPU:1, one launch (start us, length us, event | category | flops | bytes accessed | tf_op | source)
XLA Modules:
  0.0 108.6 jit_solution(16460554024423071698)
XLA Ops:
  0.6 1.1 faces_x.1
  1.7 4.9 %collective-permute-start = (bf16[25,8,128]{2,1,0:T(8,128)(2,1)S(1)}, bf16[25,8,128]{2,1,0:T(8,128)(2,1)S(1)}, u32[]{:S(2)}, u32[]{:S(2)}) collective-permute-start(bf16[25,8,128]{2,1,0:T(8,128)(2,1)S(1)} %get-tuple-element.27), channel_id=1, source_target_pairs={{8,16},{16,8},{24,32},{32,24},{40,48},{48,40},{56,64},{64,56},{72,... | collective-permute-start | bytes 153608 | tf_op jit(solution)/shard_map/ppermute | solution.py:494
  6.6 4.5 %collective-permute-start.1 = (bf16[25,8,128]{2,1,0:T(8,128)(2,1)S(1)}, bf16[25,8,128]{2,1,0:T(8,128)(2,1)S(1)}, u32[]{:S(2)}, u32[]{:S(2)}) collective-permute-start(bf16[25,8,128]{2,1,0:T(8,128)(2,1)S(1)} %get-tuple-element.28), channel_id=1, source_target_pairs={{0,8},{8,0},{16,24},{24,16},{32,40},{40,32},{48,56},{56,48},{64,72... | collective-permute-start | bytes 153608 | tf_op jit(solution)/shard_map/ppermute | solution.py:494
  11.2 0.9 collective-permute-done.1.from_a.x_a
  12.1 0.7 collective-permute-start.2
  12.8 3.5 %collective-permute-start.3 = (bf16[38,8,128]{2,1,0:T(8,128)(2,1)S(1)}, bf16[38,8,128]{2,1,0:T(8,128)(2,1)S(1)}, u32[]{:S(2)}, u32[]{:S(2)}) collective-permute-start(bf16[38,8,128]{2,1,0:T(8,128)(2,1)S(1)} %get-tuple-element.30), channel_id=1, source_target_pairs={{0,1},{1,0},{2,3},{3,2},{4,5},{5,4},{6,7},{7,6},{8,9},{9,8},{10,11... | collective-permute-start | bytes 233480 | tf_op jit(solution)/shard_map/ppermute | solution.py:494
  16.3 1.5 %weights.1 = (bf16[3456,128]{1,0:T(8,128)(2,1)S(1)}, bf16[128,3456]{1,0:T(8,128)(2,1)S(1)}) custom-call(bf16[3456,128]{1,0:T(8,128)(2,1)} %bitcast.14, bf16[27,128,128]{2,1,0:T(8,128)(2,1)} %second_weight.1), custom_call_target="tpu_custom_call" | custom-call | bytes 8000000 | tf_op jit(solution)/shard_map/weights/pallas_call | solution.py:392
  17.8 0.8 collective-permute-done.3.y_a
  18.5 5.7 %grads.1 = (bf16[28,128,128]{2,1,0:T(8,128)(2,1)S(1)}, bf16[8,8,8,128]{3,2,1,0:T(8,128)(2,1)S(1)}, bf16[2,128,512]{2,1,0:T(8,128)(2,1)S(1)}, bf16[2,512,3456]{2,1,0:T(8,128)(2,1)S(1)}) custom-call(bf16[8,8,8,128]{3,2,1,0:T(8,128)(2,1)S(1)} %get-tuple-element.22.masked, bf16[8,8,8,128]{3,2,1,0:T(8,128)(2,1)S(1)} %get-tuple-element.23.graded, ...), custom_call_target="tpu_custom_call" | custom-call | flops 1811939328 | bytes 8000000 | tf_op jit(solution)/shard_map/grads/pallas_call | solution.py:405
  24.2 2.7 %collective-permute-start.4 = (bf16[28,128,128]{2,1,0:T(8,128)(2,1)S(1)}, bf16[28,128,128]{2,1,0:T(8,128)(2,1)S(1)}, u32[]{:S(2)}, u32[]{:S(2)}) collective-permute-start(bf16[28,128,128]{2,1,0:T(8,128)(2,1)S(1)} %get-tuple-element.33), channel_id=1, source_target_pairs={{0,8},{8,0},{1,9},{9,1},{2,10},{10,2},{3,11},{11,3},{4,12},{12,4},... | collective-permute-start | bytes 2752520 | tf_op jit(solution)/shard_map/ppermute | solution.py:525
  26.9 0.8 kept.1
  27.7 1.3 %collective-permute-done.4 = bf16[28,128,128]{2,1,0:T(8,128)(2,1)S(1)} collective-permute-done((bf16[28,128,128]{2,1,0:T(8,128)(2,1)S(1)}, bf16[28,128,128]{2,1,0:T(8,128)(2,1)S(1)}, u32[]{:S(2)}, u32[]{:S(2)}) %collective-permute-start.4) | collective-permute-done | bytes 917536 | tf_op jit(solution)/shard_map/ppermute | solution.py:525
  29.0 0.2 add_convert_fusion
  29.3 28.0 %all_to_all.15 = bf16[32,112,128]{2,1,0:T(8,128)(2,1)S(1)} all-to-all(bf16[32,112,128]{2,1,0:T(8,128)(2,1)S(1)} %bitcast.13), channel_id=1, replica_groups=mesh['x_lo'=2,'z_hi'=8,'z_lo'=2,'core'=2,'x_hi'=2,'y'=4] {'x_lo','z_lo',..., dimensions={0} | all-to-all | bytes 1835008 | tf_op jit(solution)/shard_map/all_to_all | solution.py:498
  57.3 0.1 reduce_sum.21
  57.4 0.7 broadcast_in_dim.4
  58.1 7.5 %all-to-all-start.1 = ((bf16[8,112,128]{2,1,0:T(8,128)(2,1)}), bf16[8,112,128]{2,1,0:T(8,128)(2,1)S(1)}, u32[]{:S(2)}, u32[]{:S(2)}) async-start(bf16[8,112,128]{2,1,0:T(8,128)(2,1)} %broadcast_in_dim.4), calls=%async_computation.1 | async-start | bytes 458752 | tf_op jit(solution)/shard_map/all_to_all | solution.py:498
  65.7 6.9 %activations.1 = bf16[8,8,8,128]{3,2,1,0:T(8,128)(2,1)} custom-call(bf16[8,8,8,128]{3,2,1,0:T(8,128)(2,1)S(1)} %get-tuple-element.22.masked, f32[8,8,8,128]{3,2,1,0:T(8,128)S(1)} %get-tuple-element.24.masks, s32[1,27]{1,0:T(1,128)} %bitcast.22, bf16[3456,128]{1,0:T(8,128)(2,1)} %bitcast.15, bf16[3456,128]{1,0:T(8,128)(2,1)} %bitcast.16, ...), custom_call_target="tpu_custom_call" | custom-call | flops 1415577600 | bytes 2000000 | tf_op jit(solution)/shard_map/activations/pallas_call | solution.py:471
  72.6 8.7 %all-to-all-done.1 = bf16[8,112,128]{2,1,0:T(8,128)(2,1)S(1)} async-done(((bf16[8,112,128]{2,1,0:T(8,128)(2,1)}), bf16[8,112,128]{2,1,0:T(8,128)(2,1)S(1)}, u32[]{:S(2)}, u32[]{:S(2)}) %all-to-all-start.1) | async-done | bytes 229408 | tf_op jit(solution)/shard_map/all_to_all | solution.py:498
  81.4 16.9 %all_to_all.16 = bf16[32,112,128]{2,1,0:T(8,128)(2,1)S(1)} all-to-all(bf16[32,112,128]{2,1,0:T(8,128)(2,1)S(1)} %broadcast_in_dim.5), channel_id=1, replica_groups=mesh['x_lo'=2,'z_hi'=8,'z_lo'=2,'core'=2,'x_hi'=2,'y'=4] {'x_lo','z_lo',..., dimensions={0} | all-to-all | bytes 1835008 | tf_op jit(solution)/shard_map/all_to_all | solution.py:498
  98.4 7.2 %collective-permute-start.5 = (bf16[28,128,128]{2,1,0:T(8,128)(2,1)S(1)}, bf16[28,128,128]{2,1,0:T(8,128)(2,1)S(1)}, u32[]{:S(2)}, u32[]{:S(2)}) collective-permute-start(bf16[28,128,128]{2,1,0:T(8,128)(2,1)S(1)} %bitcast.11), channel_id=1, source_target_pairs={{0,8},{8,0},{1,9},{9,1},{2,10},{10,2},{3,11},{11,3},{4,12},{12,4},... | collective-permute-start | bytes 2752520 | tf_op jit(solution)/shard_map/ppermute | solution.py:533
  105.6 0.9 place_own.1
  106.6 1.1 %collective-permute-done.5.source = bf16[28,128,128]{2,1,0:T(8,128)(2,1)S(1)} collective-permute-done((bf16[28,128,128]{2,1,0:T(8,128)(2,1)S(1)}, bf16[28,128,128]{2,1,0:T(8,128)(2,1)S(1)}, u32[]{:S(2)}, u32[]{:S(2)}) %collective-permute-start.5) | collective-permute-done | bytes 917536 | tf_op jit(solution)/shard_map/ppermute | solution.py:533
  107.7 0.9 place_other.1
  (6 shorter events, 0.2 us)
Async XLA Ops:
  1.7 9.5 %collective-permute-start = (bf16[25,8,128]{2,1,0:T(8,128)(2,1)S(1)}, bf16[25,8,128]{2,1,0:T(8,128)(2,1)S(1)}, u32[]{:S(2)}, u32[]{:S(2)}) collective-permute-start(bf16[25,8,128]{2,1,0:T(8,128)(2,1)S(1)} %get-tuple-element.27), channel_id=1, source_target_pairs={{8,16},{16,8},{24,32},{32,24},{40,48},{48,40},{56,64},{64,56},{72,... | collective-permute-start | bytes 153608 | tf_op jit(solution)/shard_map/ppermute | solution.py:494
  6.6 5.4 %collective-permute-start.1 = (bf16[25,8,128]{2,1,0:T(8,128)(2,1)S(1)}, bf16[25,8,128]{2,1,0:T(8,128)(2,1)S(1)}, u32[]{:S(2)}, u32[]{:S(2)}) collective-permute-start(bf16[25,8,128]{2,1,0:T(8,128)(2,1)S(1)} %get-tuple-element.28), channel_id=1, source_target_pairs={{0,8},{8,0},{16,24},{24,16},{32,40},{40,32},{48,56},{56,48},{64,72... | collective-permute-start | bytes 153608 | tf_op jit(solution)/shard_map/ppermute | solution.py:494
  12.1 5.7 %collective-permute-start.2 = (bf16[38,8,128]{2,1,0:T(8,128)(2,1)S(1)}, bf16[38,8,128]{2,1,0:T(8,128)(2,1)S(1)}, u32[]{:S(2)}, u32[]{:S(2)}) collective-permute-start(bf16[38,8,128]{2,1,0:T(8,128)(2,1)S(1)} %get-tuple-element.29), channel_id=1, source_target_pairs={{1,2},{2,1},{3,4},{4,3},{5,6},{6,5},{9,10},{10,9},{11,12},{12,11},... | collective-permute-start | bytes 233480 | tf_op jit(solution)/shard_map/ppermute | solution.py:494
  12.8 5.8 %collective-permute-start.3 = (bf16[38,8,128]{2,1,0:T(8,128)(2,1)S(1)}, bf16[38,8,128]{2,1,0:T(8,128)(2,1)S(1)}, u32[]{:S(2)}, u32[]{:S(2)}) collective-permute-start(bf16[38,8,128]{2,1,0:T(8,128)(2,1)S(1)} %get-tuple-element.30), channel_id=1, source_target_pairs={{0,1},{1,0},{2,3},{3,2},{4,5},{5,4},{6,7},{7,6},{8,9},{9,8},{10,11... | collective-permute-start | bytes 233480 | tf_op jit(solution)/shard_map/ppermute | solution.py:494
  24.2 4.8 %collective-permute-start.4 = (bf16[28,128,128]{2,1,0:T(8,128)(2,1)S(1)}, bf16[28,128,128]{2,1,0:T(8,128)(2,1)S(1)}, u32[]{:S(2)}, u32[]{:S(2)}) collective-permute-start(bf16[28,128,128]{2,1,0:T(8,128)(2,1)S(1)} %get-tuple-element.33), channel_id=1, source_target_pairs={{0,8},{8,0},{1,9},{9,1},{2,10},{10,2},{3,11},{11,3},{4,12},{12,4},... | collective-permute-start | bytes 2752520 | tf_op jit(solution)/shard_map/ppermute | solution.py:525
  58.1 23.1 %all-to-all-start.1 = ((bf16[8,112,128]{2,1,0:T(8,128)(2,1)}), bf16[8,112,128]{2,1,0:T(8,128)(2,1)S(1)}, u32[]{:S(2)}, u32[]{:S(2)}) async-start(bf16[8,112,128]{2,1,0:T(8,128)(2,1)} %broadcast_in_dim.4), calls=%async_computation.1 | async-start | bytes 458752 | tf_op jit(solution)/shard_map/all_to_all | solution.py:498
  98.4 9.3 %collective-permute-start.5 = (bf16[28,128,128]{2,1,0:T(8,128)(2,1)S(1)}, bf16[28,128,128]{2,1,0:T(8,128)(2,1)S(1)}, u32[]{:S(2)}, u32[]{:S(2)}) collective-permute-start(bf16[28,128,128]{2,1,0:T(8,128)(2,1)S(1)} %bitcast.11), channel_id=1, source_target_pairs={{0,8},{8,0},{1,9},{9,1},{2,10},{10,2},{3,11},{11,3},{4,12},{12,4},... | collective-permute-start | bytes 2752520 | tf_op jit(solution)/shard_map/ppermute | solution.py:533

commit v5 on v4

--- a/solution.py
+++ b/solution.py
@@ -12,7 +12,7 @@
 GX = ("x_lo", "z_hi", "z_lo", "core")
 GY = ("x_hi", "y")
 NEAR = ("x_lo", "z_lo", "x_hi", "y")
-FAR = ("z_hi",)
+FAR = "z_hi"
 SWAP = [(0, 1), (1, 0)]
 F32 = jnp.float32
 BF16 = jnp.bfloat16
@@ -37,6 +37,11 @@
     return [jnp.where(neighbours[0, base + r] >= 0, 1.0, 0.0).astype(F32) for r in range(3)]
 
 
+def flags_of(tiles, p, q):
+    base = 9 * (p + 1) + 3 * (q + 1)
+    return [tiles[base + r] for r in range(3)]
+
+
 def live_of(neighbours):
     return jnp.where(neighbours[0, 13] >= 0, 1, 0)
 
@@ -56,8 +61,20 @@
         copy.wait()
 
 
-def faces_x(
-    features, cotangent, occupancy, neighbours, masked, graded, masks, out_b, out_a, own, grads, occupied, table, sems
+def swapped(face_b, face_a, axis):
+    even = is_even(axis)
+
+    def lower(tile):
+        return jnp.where(even, face_b[tile], face_a[tile])
+
+    def higher(tile):
+        return jnp.where(even, face_a[tile], face_b[tile])
+
+    return lower, higher
+
+
+def faces_y(
+    features, cotangent, occupancy, neighbours, masked, graded, masks, flags, out_b, out_a, own, grads, occupied, table, sems
 ):
     copies = start_all([
         pltpu.make_async_copy(occupancy, occupied, sems.at[0]),
@@ -65,9 +82,11 @@
         pltpu.make_async_copy(features, own, sems.at[2]),
         pltpu.make_async_copy(cotangent, grads, sems.at[3]),
     ])
-    even = is_even("core")
+    even = is_even("y")
     wait_all(copies[:2])
     live = live_of(table)
+    for n in range(27):
+        flags[n] = jnp.full((E, 128), jnp.where(table[0, n] >= 0, 1.0, 0.0), F32)
     for x in range(E):
         masks[x] = row_mask(lambda x, y: occupied[x, y] * live, x)
     wait_all(copies[2:])
@@ -75,48 +94,45 @@
         masked[x] = (own[x].astype(F32) * masks[x]).astype(BF16)
         graded[x] = (grads[x].astype(F32) * masks[x]).astype(BF16)
     rows = lax.broadcasted_iota(jnp.int32, (E, 128), 0)
-    for out, high in ((out_a, jnp.where(even, 1, 0)), (out_b, jnp.where(even, 0, 1))):
-        edge = (E - 1) * high
-        for i in range(2):
-            out[E * i : E * i + E] = masked[(E - 2) * high + i]
-        out[16:24] = graded[edge]
+    for out, high in ((out_b, jnp.where(even, 0, 1)), (out_a, jnp.where(even, 1, 0))):
+        first, edge = ((E - 2) * high, (E - 1) * high)
         values = jnp.zeros((E, 128), jnp.int32)
-        for y in range(E):
-            values = jnp.where(rows == y, occupied[edge, y] * live, values)
+        for x in range(E):
+            for i in range(2):
+                out[E * i + x] = masked[x, first + i]
+            out[16 + x] = graded[x, edge]
+            values = jnp.where(rows == x, occupied[x, edge] * live, values)
         out[24] = values.astype(F32).astype(BF16)
 
 
-def faces_y(masked, graded, masks, from_b, from_a, out_b, out_a):
-    even_x = is_even("core")
-    even = is_even("y")
+def faces_x(masked, graded, masks, y_b, y_a, out_b, out_a):
+    even = is_even("core")
+    left, right = swapped(y_b, y_a, "y")
     rows = lax.broadcasted_iota(jnp.int32, (E, 128), 0)
     weights = jnp.left_shift(jnp.ones((E, 128), jnp.int32), rows).astype(F32)
     zero = jnp.zeros((E, 128), BF16)
-    for out, high in ((out_a, jnp.where(even, 1, 0)), (out_b, jnp.where(even, 0, 1))):
+
+    def row_of(tile, row):
+        return jnp.sum(jnp.where(rows == row, tile.astype(F32), 0.0), axis=0, keepdims=True)
+
+    for out, high in ((out_b, jnp.where(even, 0, 1)), (out_a, jnp.where(even, 1, 0))):
         first, edge = ((E - 2) * high, (E - 1) * high)
         for i in range(2):
-            for x in range(E):
-                out[12 * i + 2 + x] = masked[x, first + i]
-                if i == 0:
-                    out[26 + x] = graded[x, edge]
-            for x in range(2):
-                low_a, low_b = (from_a[E * x + first + i], from_b[E * x + first + i])
-                out[12 * i + x] = jnp.where(even_x, low_b, low_a)
-                out[12 * i + E + 2 + x] = jnp.where(even_x, low_a, low_b)
-        at_a, at_b = (from_a[16 + edge], from_b[16 + edge])
+            out[12 * i + 2 : 12 * i + E + 2] = masked[first + i]
+            for y in range(2):
+                out[12 * i + y] = left(E * y + first + i)
+                out[12 * i + E + 2 + y] = right(E * y + first + i)
         out[24] = zero
+        out[25] = left(16 + edge)
+        out[26:34] = graded[edge]
+        out[34] = right(16 + edge)
         out[35] = zero
-        out[25] = jnp.where(even_x, at_b, at_a)
-        out[34] = jnp.where(even_x, at_a, at_b)
         values = jnp.zeros((E, 128), F32)
-        for x in range(E):
-            values = jnp.where(rows == x, jnp.sum(masks[x, edge] * weights, axis=0, keepdims=True), values)
+        for y in range(E):
+            values = jnp.where(rows == y, jnp.sum(masks[edge, y] * weights, axis=0, keepdims=True), values)
         out[36] = values.astype(BF16)
-        in_a, in_b = (from_a[24].astype(F32), from_b[24].astype(F32))
-        corner_a = jnp.sum(jnp.where(rows == edge, in_a, 0.0), axis=0, keepdims=True)
-        corner_b = jnp.sum(jnp.where(rows == edge, in_b, 0.0), axis=0, keepdims=True)
-        low, above = (jnp.where(even_x, corner_b, corner_a), jnp.where(even_x, corner_a, corner_b))
-        out[37] = jnp.where(rows == 0, low, jnp.where(rows == 1, above, 0.0)).astype(BF16)
+        low, high_row = (row_of(left(24), edge), row_of(right(24), edge))
+        out[37] = jnp.where(rows == 0, low, jnp.where(rows == 1, high_row, 0.0)).astype(BF16)
 
 
 def spread(store, values, flags, layers):
@@ -132,10 +148,10 @@
         store(2, d, up * jnp.where(rows == E - 1, over, own)[None])
 
 
-def spread_window(shifts, neighbours, value_of, width, layers):
+def spread_window(shifts, flags_at, value_of, width, layers):
     for p in (-1, 0, 1):
         for q in (-1, 0, 1):
-            flags = present(neighbours, p, q)
+            flags = flags_at(p, q)
             start = {-1: 0, 0: width, 1: E + width}[p]
             columns = {-1: slice(0, width), 0: slice(width, E + width), 1: slice(E + width, E + 2 * width)}[q]
 
@@ -160,10 +176,30 @@
     lax.fori_loop(0, 27, step, 0)
 
 
-def gather_own(shifts, patches, i, j, k, lanes):
-    for x in range(E):
-        part = shifts[k, i + x, pl.ds(j, E)]
-        patches[x * 64 : x * 64 + 64, lanes] = part.reshape(64, 128).astype(BF16)
+SIDE = 9 * 128
+LAYERS = (E + 2) * 64
+
+
+def gather_own(*fields):
+    def step(tap, carry):
+        lanes = pl.ds(pl.multiple_of(tap * 128, 128), 128)
+        for shifts, patches in fields:
+            for x in range(E + 2):
+                part = shifts[tap % 3, x, pl.ds(tap // 3, E)]
+                patches[x * 64 : x * 64 + 64, lanes] = part.reshape(64, 128).astype(BF16)
+        return carry
+
+    lax.fori_loop(0, 9, step, 0)
+
+
+def patch_dot(patches, weights):
+    total = None
+    for i in range(3):
+        part = jnp.dot(
+            patches[64 * i : 64 * i + 512], weights[SIDE * i : SIDE * i + SIDE], preferred_element_type=F32
+        )
+        total = part if total is None else total + part
+    return total
 
 
 def weights_kernel(first_weight, second_weight, first_taps, back_weight, second_taps, sems):
@@ -181,55 +217,48 @@
 
 
 def main_kernel(
-    masked, graded, masks, neighbours, first_taps, back_weight, x_b, x_a, y_b, y_a,
+    masked, graded, masks, flags, first_taps, back_weight, x_b, x_a, y_b, y_a,
     send, hidden_out, factors, patches,
-    shifts, grad_shifts, raw, table, sems,
+    shifts, grad_shifts, raw,
 ):
-    copies = start_all([
-        pltpu.make_async_copy(neighbours, table, sems.at[0]),
-    ])
     even_x = is_even("core")
-    even_y = is_even("y")
-    wait_all(copies)
+    below, above = swapped(x_b, x_a, "core")
+    left, right = swapped(y_b, y_a, "y")
+
+    def beside(p, q, first):
+        columns = {-1: slice(first - 1, first), 0: slice(first, first + E), 1: slice(first + E, first + E + 1)}[q]
+        return (below if p == -1 else above)(columns).astype(F32)
 
     def masked_at(p, q, x, at):
-        if q == -1:
-            return jnp.where(even_y, y_b[12 + at + 1], y_a[12 + at + 1]).astype(F32)[None]
-        if q == 1:
-            return jnp.where(even_y, y_a[at + 1], y_b[at + 1]).astype(F32)[None]
-        if p == -1:
-            return jnp.where(even_x, x_b[E : 2 * E], x_a[E : 2 * E]).astype(F32)
-        if p == 1:
-            return jnp.where(even_x, x_a[0:E], x_b[0:E]).astype(F32)
+        if p != 0:
+            return beside(p, q, 14 if p == -1 else 2)
+        if q != 0:
+            return (left(E + x) if q == -1 else right(x)).astype(F32)[None]
         return masked[x].astype(F32)
 
     def grad_at(p, q, x, at):
-        if q == -1:
-            return jnp.where(even_y, y_b[24 + at + 1], y_a[24 + at + 1]).astype(F32)[None]
-        if q == 1:
-            return jnp.where(even_y, y_a[24 + at + 1], y_b[24 + at + 1]).astype(F32)[None]
-        if p == -1:
-            return jnp.where(even_x, x_b[16:24], x_a[16:24]).astype(F32)
-        if p == 1:
-            return jnp.where(even_x, x_a[16:24], x_b[16:24]).astype(F32)
+        if p != 0:
+            return beside(p, q, 26)
+        if q != 0:
+            return (left if q == -1 else right)(16 + x).astype(F32)[None]
         return graded[x].astype(F32)
 
-    spread_window(shifts, table, masked_at, 1, (0,))
-    spread_window(grad_shifts, table, grad_at, 1, (0,))
-
-    def fill(tap, i, j, k, lanes):
-        gather_own(shifts, patches.at[0], i, j, k, lanes)
-        gather_own(grad_shifts, patches.at[1], i, j, k, lanes)
-
-    for_each_tap(fill)
-
-    pre = jnp.dot(patches[0], first_taps[...], preferred_element_type=F32)
+    spread_window(shifts, lambda p, q: flags_of(flags, p, q), masked_at, 1, (0,))
+    spread_window(grad_shifts, lambda p, q: flags_of(flags, p, q), grad_at, 1, (0,))
+
+    gather_own((shifts, patches.at[0]), (grad_shifts, patches.at[1]))
+
+    pre = patch_dot(patches.at[0], first_taps)
     logistic = jax.nn.sigmoid(pre)
     mask = masks[...].reshape(512, 128)
     hidden = (pre * logistic * mask).astype(BF16)
     hidden_out[...] = hidden.reshape(E, E, E, 128)
-    back = lax.dot_general(
-        patches[1], back_weight[...], (((1,), (1,)), ((), ())), preferred_element_type=F32
+    back = sum(
+        lax.dot_general(
+            patches[1, 64 * i : 64 * i + 512], back_weight[:, SIDE * i : SIDE * i + SIDE],
+            (((1,), (1,)), ((), ())), preferred_element_type=F32,
+        )
+        for i in range(3)
     )
     grad_pre = (back * (logistic * (1.0 + pre * (1.0 - logistic))) * mask).astype(BF16)
     factors[0] = grad_pre.astype(F32).T.astype(BF16)
@@ -242,7 +271,10 @@
 
 
 def taps_of(factors, patches, which, out, raw):
-    raw[...] = jnp.dot(factors[which], patches[which], preferred_element_type=F32)
+    for i in range(3):
+        raw[:, SIDE * i : SIDE * i + SIDE] = jnp.dot(
+            factors[which], patches[which, 64 * i : 64 * i + 512], preferred_element_type=F32
+        )
 
     @pl.when(which == 0)
     def _():
@@ -267,20 +299,8 @@
         pltpu.make_async_copy(first_weight, first_taps, sems.at[1]),
         pltpu.make_async_copy(second_weight, second_taps, sems.at[2]),
     ])
-    even_x = is_even("core")
-    even_y = is_even("y")
-
-    def below(tiles):
-        return jnp.where(even_x, x_b[tiles], x_a[tiles]).astype(F32)
-
-    def above(tiles):
-        return jnp.where(even_x, x_a[tiles], x_b[tiles]).astype(F32)
-
-    def left(tiles):
-        return jnp.where(even_y, y_b[tiles], y_a[tiles]).astype(F32)
-
-    def right(tiles):
-        return jnp.where(even_y, y_a[tiles], y_b[tiles]).astype(F32)
+    below, above = swapped(x_b, x_a, "core")
+    left, right = swapped(y_b, y_a, "y")
 
     def mask_of(tile, row):
         return bits_of(jnp.broadcast_to(tile[row : row + 1], (E, 128)).astype(jnp.int32))
@@ -288,14 +308,15 @@
     wait_all(copies[:1])
 
     def masked_at(p, q, x, at):
+        if p != 0:
+            first, count = {-1: (0, 2), 0: (2, E), 1: (E + 2, 2)}[q]
+            return (below if p == -1 else above)(pl.ds(12 * x + first, count)).astype(F32)
         if q != 0:
             side = left if q == -1 else right
-            return jnp.stack([side(at), side(12 + at)])
-        if p != 0:
-            return (below if p == -1 else above)(pl.ds(E * x, E))
+            return jnp.stack([side(x), side(E + x)]).astype(F32)
         return masked[x].astype(F32)
 
-    spread_window(wide, table, masked_at, 2, (-1, 0, 1))
+    spread_window(wide, lambda p, q: present(table, p, q), masked_at, 2, (-1, 0, 1))
 
     def layer_of(p, q):
         flags = present(table, p, q)
@@ -322,28 +343,29 @@
     wait_all(copies[1:])
 
     ring = jax.nn.silu(jnp.dot(ring_patches[...], first_taps[...], preferred_element_type=F32))
-    low, high = (below(24), above(24))
-    sides = [(side(36), side(37)) for side in (left, right)]
+    ends = [(end(36).astype(F32), end(37).astype(F32)) for end in (below, above)]
+    sides = [side(24).astype(F32) for side in (left, right)]
     for y in range(E):
-        hidden[0, y + 1] = (ring[8 * y : 8 * y + 8] * mask_of(low, y)).astype(BF16).astype(F32)
-        hidden[E + 1, y + 1] = (ring[64 + 8 * y : 72 + 8 * y] * mask_of(high, y)).astype(BF16).astype(F32)
+        for m, x in enumerate((0, E + 1)):
+            part = ring[64 * m + 8 * y : 64 * m + 8 * y + 8] * mask_of(ends[m][0], y)
+            hidden[x, y + 1] = part.astype(BF16).astype(F32)
     for x in range(E):
         hidden[x + 1, 1 : E + 1] = hidden_own[x].astype(F32)
         for n, y in enumerate((0, E + 1)):
-            part = ring[128 + 64 * n + 8 * x : 136 + 64 * n + 8 * x] * mask_of(sides[n][0], x)
+            part = ring[128 + 64 * n + 8 * x : 136 + 64 * n + 8 * x] * mask_of(sides[n], x)
             hidden[x + 1, y] = part.astype(BF16).astype(F32)
     for m, x in enumerate((0, E + 1)):
         for n, y in enumerate((0, E + 1)):
             at = 256 + 16 * m + 8 * n
-            hidden[x, y] = (ring[at : at + 8] * mask_of(sides[n][1], m)).astype(BF16).astype(F32)
+            hidden[x, y] = (ring[at : at + 8] * mask_of(ends[m][1], n)).astype(BF16).astype(F32)
 
     def hidden_at(p, q, x, at):
         columns = {-1: slice(0, 1), 0: slice(1, E + 1), 1: slice(E + 1, E + 2)}[q]
         return hidden[at, columns]
 
-    spread_window(shifts, table, hidden_at, 1, (0,))
-    for_each_tap(lambda tap, i, j, k, lanes: gather_own(shifts, patches, i, j, k, lanes))
-    result = jnp.dot(patches[...], second_taps[...], preferred_element_type=F32)
+    spread_window(shifts, lambda p, q: present(table, p, q), hidden_at, 1, (0,))
+    gather_own((shifts, patches))
+    result = patch_dot(patches, second_taps)
     for x in range(E):
         part = result[64 * x : 64 * x + 64].reshape(E, E, 128) * masks[x]
         activations[x] = part.astype(BF16)
@@ -365,26 +387,26 @@
     return pltpu.with_memory_space_constraint(array, pltpu.HBM)
 
 
-def local_faces_x(features, cotangent, occupancy, neighbours):
+def local_faces_y(features, cotangent, occupancy, neighbours):
     face, field = (shape(25, E, 128), shape(E, E, E, 128))
     return pl.pallas_call(
-        faces_x,
-        out_shape=(field, field, shape(E, E, E, 128, dtype=F32), face, face),
+        faces_y,
+        out_shape=(field, field, shape(E, E, E, 128, dtype=F32), shape(27, E, 128, dtype=F32), face, face),
         in_specs=[HBM] * 4,
-        out_specs=(VMEM,) * 5,
+        out_specs=(VMEM,) * 6,
         scratch_shapes=[
             vmem(E, E, E, 128), vmem(E, E, E, 128), pltpu.SMEM((E, E), jnp.int32), pltpu.SMEM((1, 27), jnp.int32),
             pltpu.SemaphoreType.DMA((4,)),
         ],
+        compiler_params=params(), name="faces_y",
+    )(*map(held, (features, cotangent, occupancy, neighbours)))
+
+
+def local_faces_x(*operands):
+    face = shape(38, E, 128)
+    return pl.pallas_call(
+        faces_x, out_shape=(face, face), in_specs=[VMEM] * 5, out_specs=(VMEM, VMEM),
         compiler_params=params(), name="faces_x",
-    )(*map(held, (features, cotangent, occupancy, neighbours)))
-
-
-def local_faces_y(*operands):
-    face = shape(38, E, 128)
-    return pl.pallas_call(
-        faces_y, out_shape=(face, face), in_specs=[VMEM] * 5, out_specs=(VMEM, VMEM),
-        compiler_params=params(), name="faces_y",
     )(*operands)
 
 
@@ -405,14 +427,13 @@
     return pl.pallas_call(
         main_kernel,
         out_shape=(
-            shape(28, 128, 128), shape(E, E, E, 128), shape(2, 128, 512), shape(2, 512, 27 * 128)
+            shape(28, 128, 128), shape(E, E, E, 128), shape(2, 128, 512), shape(2, LAYERS, SIDE)
         ),
-        in_specs=[VMEM] * 3 + [HBM] + [VMEM] * 6,
+        in_specs=[VMEM] * 10,
         out_specs=(VMEM,) * 4,
         scratch_shapes=[
             vmem(3, E + 2, E + 2, E, 128, dtype=F32), vmem(3, E + 2, E + 2, E, 128, dtype=F32),
             vmem(128, 27 * 128, dtype=F32),
-            pltpu.SMEM((1, 27), jnp.int32), pltpu.SemaphoreType.DMA((1,)),
         ],
         compiler_params=params(),
         cost_estimate=pl.CostEstimate(flops=8 * 512 * 3456 * 128, bytes_accessed=8000000, transcendentals=100000),
@@ -467,6 +488,27 @@
     )(source, *outs)
 
 
+def fold_kernel(parts, out):
+    for row in range(0, parts.shape[1], 16):
+        rows = slice(row, row + 16)
+        total = parts[0, rows].astype(F32)
+        for i in range(1, parts.shape[0]):
+            total = total + parts[i, rows].astype(F32)
+        for i in range(out.shape[0]):
+            out[i, rows] = total.astype(BF16)
+
+
+def local_fold(parts, count):
+    return pl.pallas_call(
+        fold_kernel,
+        out_shape=shape(count, *parts.shape[1:]),
+        in_specs=[VMEM],
+        out_specs=VMEM,
+        compiler_params=params(),
+        name="fold",
+    )(parts)
+
+
 def local_last(*operands):
     return pl.pallas_call(
         last_kernel,
@@ -478,7 +520,7 @@
             vmem(3, E + 4, E + 4, 3, E, 128, dtype=F32),
             vmem(E + 2, E + 2, E, 128, dtype=F32),
             vmem(3, E + 2, E + 2, E, 128, dtype=F32),
-            vmem(288, 27 * 128), vmem(512, 27 * 128),
+            vmem(288, 27 * 128), vmem(LAYERS, SIDE),
             pltpu.SMEM((1, 27), jnp.int32), pltpu.SemaphoreType.DMA((3,)),
         ],
         compiler_params=params(),
@@ -510,12 +552,14 @@
     features, cotangent = (array.reshape(E, E, E, 128) for array in (features, cotangent))
     occupancy, neighbours = (occupancy.reshape(E, E), neighbours.reshape(1, 27))
     first_taps, second_taps = (weight.reshape(27 * 128, 128) for weight in (first_weight, second_weight))
-    masked, graded, masks, *out = local_faces_x(features, cotangent, occupancy, neighbours)
-    x_b, x_a = paired(*out, GX)
-    y_b, y_a = paired(*local_faces_y(masked, graded, masks, x_b, x_a), GY)
+    masked, graded, masks, flags, *out = local_faces_y(features, cotangent, occupancy, neighbours)
+    y_b, y_a = paired(*out, GY)
+    weights = local_weights(first_taps, second_weight)
+    y_b, y_a, *weights = lax.optimization_barrier((y_b, y_a, *weights))
+    x_b, x_a = paired(*local_faces_x(masked, graded, masks, y_b, y_a), GX)
     faces = (x_b, x_a, y_b, y_a)
     send, hidden, factors, patches = local_main(
-        masked, graded, masks, held(neighbours), *local_weights(first_taps, second_weight), *faces
+        masked, graded, masks, flags, *weights, *faces
     )
     activations = local_last(
         masked, masks, *map(held, (neighbours, first_taps, second_taps)), *faces, hidden
@@ -525,8 +569,9 @@
     got = lax.ppermute(send, "core", SWAP)
     keep = local_keep(factors, patches)
     half = (keep + got.astype(F32)).astype(BF16)
-    part = summed(exchange(half.reshape(near, -1, 128), NEAR)).astype(BF16)
-    part = summed(exchange(shared(part, far), FAR))
+    parts = local_fold(exchange(half.reshape(near, -1, 128), NEAR), far)
+    order = [(i + far // 2) % far for i in range(far)]
+    part = summed(lax.all_to_all(parts, FAR, 0, 0, axis_index_groups=[order], tiled=True))
     part, activations = lax.optimization_barrier((part, activations))
     part = (part * scale).astype(BF16)
     half = exchange(shared(part, near), NEAR).reshape(28, 128, 128)

time: 109 us -> 103 us (0.945)
  waiting for transfers between devices: 12.7 us -> 5.74 us
  starting transfers between devices: 31.1 us -> 33 us
  Pallas kernels: 17.8 us -> 16.2 us
  blocking collectives: 45 us -> 46.5 us
    all_to_all x1, waiting for transfers between devices: 8.69 us -> 1.98 us  [local(): lax.all_to_all(parts, FAR, 0, 0, axis_index_groups=[order], tiled=True)]
    all_to_all x1, starting transfers between devices: 7.51 us -> 11.5 us  [local(): lax.all_to_all(parts, FAR, 0, 0, axis_index_groups=[order], tiled=True)]
    ppermute x1, starting transfers between devices: 7.25 us -> 5.09 us  [local(): other = lax.ppermute(half, 'core', SWAP)]
    pallas_call x1, Pallas kernels: 5.65 us -> 3.98 us  [local_main(): pl.pallas_call(main_kernel, out_shape=(shape(28, 128, 128), shape(E, E, E...]
    all_to_all x2, blocking collectives: 45 us -> 46.5 us  [exchange(): return lax.all_to_all(parts, axes, 0, 0, tiled=True)]
  transfers between devices with their start and end apart: 7 -> 7, of which waited for: 5 -> 4; matrix products, arithmetic and copies ran while one was open for 0% -> 0% of each run, Pallas kernels for 9% -> 9%
where the time goes in v5:
time: 103 us
  blocking collectives  46.5 us (45%)
  starting transfers between devices  33 us (32%)
  Pallas kernels  16.2 us (16%)
  waiting for transfers between devices  5.74 us (6%)
    all_to_all x2, blocking collectives, exchange(): return lax.all_to_all(parts, axes, 0, 0, tiled=True)  46.5 us
    all_to_all x1, starting transfers between devices, local(): lax.all_to_all(parts, FAR, 0, 0, axis_index_groups=[order], tiled=True)  11.5 us
    ppermute x2, starting transfers between devices, paired(): lax.ppermute(out_a, axis, pairs_a)  8.71 us
    pallas_call x1, Pallas kernels, local_last(): pl.pallas_call(last_kernel, out_shape=shape(E, E, E, 128), in_specs=[VMEM...  6.12 us
    ppermute x2, starting transfers between devices, paired(): lax.ppermute(out_b, axis, pairs_b)  5.87 us
    ppermute x1, starting transfers between devices, local(): other = lax.ppermute(half, 'core', SWAP)  5.09 us
    pallas_call x1, Pallas kernels, local_main(): pl.pallas_call(main_kernel, out_shape=(shape(28, 128, 128), shape(E, E, E...  3.98 us
  transfers between devices with their start and end apart: 7, of which 4 were waited for; matrix products, arithmetic and copies ran while one was open for 0% of the time, Pallas kernels for 9%

profile of v5, /device:TPU:1, one launch (start us, length us, event | category | flops | bytes accessed | tf_op | source)
XLA Modules:
  0.0 102.7 jit_solution(67219204547230683)
XLA Ops:
  0.6 1.1 %faces_y.1 = (bf16[8,8,8,128]{3,2,1,0:T(8,128)(2,1)S(1)}, bf16[8,8,8,128]{3,2,1,0:T(8,128)(2,1)S(1)}, f32[8,8,8,128]{3,2,1,0:T(8,128)S(1)}, f32[27,8,128]{2,1,0:...) custom-call(bf16[8,8,8,128]{3,2,1,0:T(8,128)(2,1)} %bitcast.17, ...), custom_call_target="tpu_custom_call" | custom-call | tf_op jit(solution)/shard_map/faces_y/pallas_call | solution.py:392
  1.7 0.7 collective-permute-start
  2.4 6.6 %collective-permute-start.1 = (bf16[25,8,128]{2,1,0:T(8,128)(2,1)S(1)}, bf16[25,8,128]{2,1,0:T(8,128)(2,1)S(1)}, u32[]{:S(2)}, u32[]{:S(2)}) collective-permute-start(bf16[25,8,128]{2,1,0:T(8,128)(2,1)S(1)} %get-tuple-element.32), channel_id=1, source_target_pairs={{0,1},{1,0},{2,3},{3,2},{4,5},{5,4},{6,7},{7,6},{8,9},{9,8},{10,11... | collective-permute-start | bytes 153608 | tf_op jit(solution)/shard_map/ppermute | solution.py:536
  9.0 1.5 %weights.1 = (bf16[3456,128]{1,0:T(8,128)(2,1)S(1)}, bf16[128,3456]{1,0:T(8,128)(2,1)S(1)}) custom-call(bf16[3456,128]{1,0:T(8,128)(2,1)} %bitcast.14, bf16[27,128,128]{2,1,0:T(8,128)(2,1)} %second_weight.1), custom_call_target="tpu_custom_call" | custom-call | bytes 8000000 | tf_op jit(solution)/shard_map/weights/pallas_call | solution.py:414
  10.5 0.1 faces_x.1
  10.5 5.2 %collective-permute-start.2 = (bf16[38,8,128]{2,1,0:T(8,128)(2,1)S(1)}, bf16[38,8,128]{2,1,0:T(8,128)(2,1)S(1)}, u32[]{:S(2)}, u32[]{:S(2)}) collective-permute-start(bf16[38,8,128]{2,1,0:T(8,128)(2,1)S(1)} %get-tuple-element.39), channel_id=1, source_target_pairs={{8,16},{16,8},{24,32},{32,24},{40,48},{48,40},{56,64},{64,56},{72,... | collective-permute-start | bytes 233480 | tf_op jit(solution)/shard_map/ppermute | solution.py:536
  15.8 2.1 %collective-permute-start.3 = (bf16[38,8,128]{2,1,0:T(8,128)(2,1)S(1)}, bf16[38,8,128]{2,1,0:T(8,128)(2,1)S(1)}, u32[]{:S(2)}, u32[]{:S(2)}) collective-permute-start(bf16[38,8,128]{2,1,0:T(8,128)(2,1)S(1)} %get-tuple-element.40), channel_id=1, source_target_pairs={{0,8},{8,0},{16,24},{24,16},{32,40},{40,32},{48,56},{56,48},{64,72... | collective-permute-start | bytes 233480 | tf_op jit(solution)/shard_map/ppermute | solution.py:536
  17.9 1.0 collective-permute-done.3.x_a
  18.9 4.0 %grads.1 = (bf16[28,128,128]{2,1,0:T(8,128)(2,1)S(1)}, bf16[8,8,8,128]{3,2,1,0:T(8,128)(2,1)S(1)}, bf16[2,128,512]{2,1,0:T(8,128)(2,1)S(1)}, bf16[2,640,1152]{2,1,0:T(8,128)(2,1)S(1)}) custom-call(bf16[8,8,8,128]{3,2,1,0:T(8,128)(2,1)S(1)} %get-tuple-element.27.masked, bf16[8,8,8,128]{3,2,1,0:T(8,128)(2,1)S(1)} %get-tuple-element.28.graded, ...), custom_call_target="tpu_custom_call" | custom-call | flops 1811939328 | bytes 8000000 | tf_op jit(solution)/shard_map/grads/pallas_call | solution.py:427
  22.9 1.9 %collective-permute-start.4 = (bf16[28,128,128]{2,1,0:T(8,128)(2,1)S(1)}, bf16[28,128,128]{2,1,0:T(8,128)(2,1)S(1)}, u32[]{:S(2)}, u32[]{:S(2)}) collective-permute-start(bf16[28,128,128]{2,1,0:T(8,128)(2,1)S(1)} %get-tuple-element.43), channel_id=1, source_target_pairs={{0,8},{8,0},{1,9},{9,1},{2,10},{10,2},{3,11},{11,3},{4,12},{12,4},... | collective-permute-start | bytes 2752520 | tf_op jit(solution)/shard_map/ppermute | solution.py:569
  24.9 0.8 kept.1
  25.7 1.6 %collective-permute-done.4 = bf16[28,128,128]{2,1,0:T(8,128)(2,1)S(1)} collective-permute-done((bf16[28,128,128]{2,1,0:T(8,128)(2,1)S(1)}, bf16[28,128,128]{2,1,0:T(8,128)(2,1)S(1)}, u32[]{:S(2)}, u32[]{:S(2)}) %collective-permute-start.4) | collective-permute-done | bytes 917536 | tf_op jit(solution)/shard_map/ppermute | solution.py:569
  27.3 0.3 add_convert_fusion
  27.6 27.7 %all_to_all.15.parts = bf16[32,112,128]{2,1,0:T(8,128)(2,1)S(1)} all-to-all(bf16[32,112,128]{2,1,0:T(8,128)(2,1)S(1)} %bitcast.13), channel_id=1, replica_groups=mesh['x_lo'=2,'z_hi'=8,'z_lo'=2,'core'=2,'x_hi'=2,'y'=4] {'x_lo','z_lo',..., dimensions={0} | all-to-all | bytes 1835008 | tf_op jit(solution)/shard_map/all_to_all | solution.py:540
  55.3 0.8 fold.1
  56.1 11.5 %all-to-all-start.1 = ((bf16[8,112,128]{2,1,0:T(8,128)(2,1)}), bf16[8,112,128]{2,1,0:T(8,128)(2,1)S(1)}, u32[]{:S(2)}, u32[]{:S(2)}) async-start(bf16[8,112,128]{2,1,0:T(8,128)(2,1)} %fold.1), calls=%async_computation.1 | async-start | bytes 458752 | tf_op jit(solution)/shard_map/all_to_all | solution.py:574
  67.6 6.1 %activations.1 = bf16[8,8,8,128]{3,2,1,0:T(8,128)(2,1)} custom-call(bf16[8,8,8,128]{3,2,1,0:T(8,128)(2,1)S(1)} %get-tuple-element.27.masked, f32[8,8,8,128]{3,2,1,0:T(8,128)S(1)} %get-tuple-element.29.masks, s32[1,27]{1,0:T(1,128)} %bitcast.21, bf16[3456,128]{1,0:T(8,128)(2,1)} %bitcast.15, bf16[3456,128]{1,0:T(8,128)(2,1)} %bitcast.16, ...), custom_call_target="tpu_custom_call" | custom-call | flops 1415577600 | bytes 2000000 | tf_op jit(solution)/shard_map/activations/pallas_call | solution.py:513
  73.7 2.0 %all-to-all-done.1 = bf16[8,112,128]{2,1,0:T(8,128)(2,1)S(1)} async-done(((bf16[8,112,128]{2,1,0:T(8,128)(2,1)}), bf16[8,112,128]{2,1,0:T(8,128)(2,1)S(1)}, u32[]{:S(2)}, u32[]{:S(2)}) %all-to-all-start.1) | async-done | bytes 229408 | tf_op jit(solution)/shard_map/all_to_all | solution.py:574
  75.7 0.1 broadcast_in_dim.2
  75.8 18.8 %all_to_all.16 = bf16[32,112,128]{2,1,0:T(8,128)(2,1)S(1)} all-to-all(bf16[32,112,128]{2,1,0:T(8,128)(2,1)S(1)} %broadcast_in_dim.2), channel_id=1, replica_groups=mesh['x_lo'=2,'z_hi'=8,'z_lo'=2,'core'=2,'x_hi'=2,'y'=4] {'x_lo','z_lo',..., dimensions={0} | all-to-all | bytes 1835008 | tf_op jit(solution)/shard_map/all_to_all | solution.py:540
  94.6 5.1 %collective-permute-start.5 = (bf16[28,128,128]{2,1,0:T(8,128)(2,1)S(1)}, bf16[28,128,128]{2,1,0:T(8,128)(2,1)S(1)}, u32[]{:S(2)}, u32[]{:S(2)}) collective-permute-start(bf16[28,128,128]{2,1,0:T(8,128)(2,1)S(1)} %bitcast.11), channel_id=1, source_target_pairs={{0,8},{8,0},{1,9},{9,1},{2,10},{10,2},{3,11},{11,3},{4,12},{12,4},... | collective-permute-start | bytes 2752520 | tf_op jit(solution)/shard_map/ppermute | solution.py:578
  99.7 0.9 place_own.1
  100.7 1.1 %collective-permute-done.5.source = bf16[28,128,128]{2,1,0:T(8,128)(2,1)S(1)} collective-permute-done((bf16[28,128,128]{2,1,0:T(8,128)(2,1)S(1)}, bf16[28,128,128]{2,1,0:T(8,128)(2,1)S(1)}, u32[]{:S(2)}, u32[]{:S(2)}) %collective-permute-start.5) | collective-permute-done | bytes 917536 | tf_op jit(solution)/shard_map/ppermute | solution.py:578
  101.8 0.9 place_other.1
  (5 shorter events, 0.0 us)
Async XLA Ops:
  1.7 8.8 %collective-permute-start = (bf16[25,8,128]{2,1,0:T(8,128)(2,1)S(1)}, bf16[25,8,128]{2,1,0:T(8,128)(2,1)S(1)}, u32[]{:S(2)}, u32[]{:S(2)}) collective-permute-start(bf16[25,8,128]{2,1,0:T(8,128)(2,1)S(1)} %get-tuple-element.31), channel_id=1, source_target_pairs={{1,2},{2,1},{3,4},{4,3},{5,6},{6,5},{9,10},{10,9},{11,12},{12,11},... | collective-permute-start | bytes 153608 | tf_op jit(solution)/shard_map/ppermute | solution.py:536
  2.4 8.1 %collective-permute-start.1 = (bf16[25,8,128]{2,1,0:T(8,128)(2,1)S(1)}, bf16[25,8,128]{2,1,0:T(8,128)(2,1)S(1)}, u32[]{:S(2)}, u32[]{:S(2)}) collective-permute-start(bf16[25,8,128]{2,1,0:T(8,128)(2,1)S(1)} %get-tuple-element.32), channel_id=1, source_target_pairs={{0,1},{1,0},{2,3},{3,2},{4,5},{5,4},{6,7},{7,6},{8,9},{9,8},{10,11... | collective-permute-start | bytes 153608 | tf_op jit(solution)/shard_map/ppermute | solution.py:536
  10.5 7.4 %collective-permute-start.2 = (bf16[38,8,128]{2,1,0:T(8,128)(2,1)S(1)}, bf16[38,8,128]{2,1,0:T(8,128)(2,1)S(1)}, u32[]{:S(2)}, u32[]{:S(2)}) collective-permute-start(bf16[38,8,128]{2,1,0:T(8,128)(2,1)S(1)} %get-tuple-element.39), channel_id=1, source_target_pairs={{8,16},{16,8},{24,32},{32,24},{40,48},{48,40},{56,64},{64,56},{72,... | collective-permute-start | bytes 233480 | tf_op jit(solution)/shard_map/ppermute | solution.py:536
  15.8 3.2 %collective-permute-start.3 = (bf16[38,8,128]{2,1,0:T(8,128)(2,1)S(1)}, bf16[38,8,128]{2,1,0:T(8,128)(2,1)S(1)}, u32[]{:S(2)}, u32[]{:S(2)}) collective-permute-start(bf16[38,8,128]{2,1,0:T(8,128)(2,1)S(1)} %get-tuple-element.40), channel_id=1, source_target_pairs={{0,8},{8,0},{16,24},{24,16},{32,40},{40,32},{48,56},{56,48},{64,72... | collective-permute-start | bytes 233480 | tf_op jit(solution)/shard_map/ppermute | solution.py:536
  22.9 4.4 %collective-permute-start.4 = (bf16[28,128,128]{2,1,0:T(8,128)(2,1)S(1)}, bf16[28,128,128]{2,1,0:T(8,128)(2,1)S(1)}, u32[]{:S(2)}, u32[]{:S(2)}) collective-permute-start(bf16[28,128,128]{2,1,0:T(8,128)(2,1)S(1)} %get-tuple-element.43), channel_id=1, source_target_pairs={{0,8},{8,0},{1,9},{9,1},{2,10},{10,2},{3,11},{11,3},{4,12},{12,4},... | collective-permute-start | bytes 2752520 | tf_op jit(solution)/shard_map/ppermute | solution.py:569
  56.1 19.6 %all-to-all-start.1 = ((bf16[8,112,128]{2,1,0:T(8,128)(2,1)}), bf16[8,112,128]{2,1,0:T(8,128)(2,1)S(1)}, u32[]{:S(2)}, u32[]{:S(2)}) async-start(bf16[8,112,128]{2,1,0:T(8,128)(2,1)} %fold.1), calls=%async_computation.1 | async-start | bytes 458752 | tf_op jit(solution)/shard_map/all_to_all | solution.py:574
  94.6 7.2 %collective-permute-start.5 = (bf16[28,128,128]{2,1,0:T(8,128)(2,1)S(1)}, bf16[28,128,128]{2,1,0:T(8,128)(2,1)S(1)}, u32[]{:S(2)}, u32[]{:S(2)}) collective-permute-start(bf16[28,128,128]{2,1,0:T(8,128)(2,1)S(1)} %bitcast.11), channel_id=1, source_target_pairs={{0,8},{8,0},{1,9},{9,1},{2,10},{10,2},{3,11},{11,3},{4,12},{12,4},... | collective-permute-start | bytes 2752520 | tf_op jit(solution)/shard_map/ppermute | solution.py:578
